TPU v7x, 512 devices: a whole 4x4x16 slice. The times are simulated.
512 devices in a mesh: gx: 16 (over y, x_hi, core), gy: 32 (over z, x_lo).
Axes of the slice: x: 4 (x_hi: 2, x_lo: 2; x = x_hi * 2 + x_lo), y: 4, z: 16, core: 2. Of those that a mesh axis runs over, the one named last changes fastest.
Arguments:
- features: bfloat16 [65536, 128], P(('gx', 'gy'))
- positions: float32 [3, 65536], P(None, ('gx', 'gy')), as said below
- wave_vectors: int32 [3, 16384], replicated, may hold values from -24 to 24, as said below
- filter_width: float32 [16], replicated, may hold values from 0.002 to 0.02
- w_charge: bfloat16 [128, 16], replicated, may hold values from -0.5 to 0.5
- w_filter_in: bfloat16 [20, 128], replicated, may hold values from -1.25 to 1.25
- filter_output_weight: bfloat16 [128, 128], replicated, may hold values from -0.5 to 0.5
- update_weight: bfloat16 [128, 128], replicated, may hold values from -0.125 to 0.125
- w_long: float32 [16, 128], replicated, may hold values from -1.5 to 1.5
- send_along_x: int32 [2, 16384], P(None, ('gx', 'gy')), may hold values from 0 to 127, as said below
- send_along_y: int32 [2, 16384], P(None, ('gx', 'gy')), may hold values from 0 to 191, as said below
- neighbours: int32 [64, 65536], P(None, ('gx', 'gy')), may hold values from 0 to 255
- neighbour_count: int32 [65536], P(('gx', 'gy')), may hold values from 8 to 64, as said below
- distances: float32 [64, 65536], P(None, ('gx', 'gy')), may hold values from 0.8 to 4.8
Outputs:
- updated: bfloat16 [65536, 128], P(('gx', 'gy'))
- forces: float32 [3, 65536], P(None, ('gx', 'gy'))
Inputs may be any that keep to these rules, and one draw needn't show every extreme that they name: `positions`: fractional coordinates; atom i lies inside the x-y cell of its domain, z below one half. `wave_vectors`: distinct integer triples with a first component of 1 to 24 and the others from -24 to 23. `send_along_x`: each list of a domain holds 32 distinct atoms of that domain. `send_along_y`: each list of a domain holds 32 distinct rows of that domain's first_table. `neighbours`: rows of the ghost table of the atom's domain; slots at or past neighbour_count are unused. `neighbour_count`: every domain has an atom with all 64 slots used.
All inputs are finite; a program needn't handle non-finite values.
Results may differ from a plain program's by a relative error of at most 0.0062.
Values may be sent and summed in bfloat16 or wider, within the bound.
A program may use at most 128 MiB of HBM per device.

v0:
```python
import math

import jax
import jax.numpy as jnp
from jax import lax
from jax.sharding import PartitionSpec as P

two_pi = 2.0 * math.pi
force_unit = 0.001


def passed_along(block, axis, distance):
    devices = range(lax.axis_size(axis))
    route = [((i - distance) % len(devices), i) for i in devices]
    return lax.ppermute(block, axis, route)


def shifted_softplus(value):
    return jax.nn.softplus(value) - math.log(2.0)


def phase_table(k_piece, coords):
    kf = k_piece.astype(jnp.float32)
    angle = two_pi * (
        kf[0][:, None] * coords[0][None, :]
        + kf[1][:, None] * coords[1][None, :]
        + kf[2][:, None] * coords[2][None, :]
    )
    return jnp.stack([jnp.cos(angle), jnp.sin(angle)]).astype(jnp.bfloat16)


def filter_structure(structure, k_piece, filter_width):
    kf = k_piece.astype(jnp.float32)
    squared = two_pi * two_pi * (kf[0] * kf[0] + kf[1] * kf[1] + 0.25 * kf[2] * kf[2])
    weight = (
        jnp.exp(-0.5 * (filter_width * filter_width)[:, None] * squared[None, :])
        * (two_pi * two_pi / squared)[None, :]
    )
    return structure * weight[:, None, :]


def expand_filtered(filtered, k_piece):
    kf = k_piece.astype(jnp.float32)
    pieces = [filtered]
    for axis_index in range(3):
        factor = two_pi * kf[axis_index]
        pieces.append(jnp.stack([factor * filtered[:, 1], -factor * filtered[:, 0]], axis=1))
    return jnp.concatenate(pieces, axis=0).astype(jnp.bfloat16)


def build_coefficients(structure, k_piece, filter_width):
    return expand_filtered(filter_structure(structure, k_piece, filter_width), k_piece)


def project(coefficient_piece, k_piece, coords):
    wave_table = phase_table(k_piece, coords)
    return jnp.einsum(
        "rpk,pka->ra", coefficient_piece, wave_table, preferred_element_type=jnp.float32
    )


def per_device(
    features,
    positions,
    wave_vectors,
    filter_width,
    w_charge,
    w_filter_in,
    filter_output_weight,
    update_weight,
    w_long,
    send_along_x,
    send_along_y,
    neighbours,
    neighbour_count,
    distances,
):
    atom_rows = features.shape[0]
    channels = w_charge.shape[1]
    wave_total = wave_vectors.shape[1]
    devices = lax.axis_size("gx") * lax.axis_size("gy")
    charges = jnp.dot(features, w_charge, preferred_element_type=jnp.float32).astype(jnp.bfloat16).T
    totals = lax.psum(jnp.sum(charges.astype(jnp.float32), axis=1), ("gx", "gy"))
    mean_charge = totals / (atom_rows * devices)
    k_block = math.gcd(wave_total, 2048)
    k_turns = wave_total // k_block
    extended = jnp.concatenate([charges, jnp.ones((1, atom_rows), jnp.bfloat16)], axis=0)

    def forward(turn_index, raw):
        k_piece = lax.dynamic_slice_in_dim(wave_vectors, turn_index * k_block, k_block, 1)
        wave_table = phase_table(k_piece, positions)
        partial_sum = jnp.einsum(
            "ca,pka->cpk", extended, wave_table, preferred_element_type=jnp.float32
        )
        return lax.dynamic_update_slice_in_dim(raw, partial_sum, turn_index * k_block, 2)

    raw = lax.fori_loop(0, k_turns, forward, jnp.zeros((channels + 1, 2, wave_total), jnp.float32))
    terms = raw[:channels] - mean_charge[:, None, None] * raw[channels][None]
    summed = lax.psum(terms, ("gx", "gy"))
    empty_fields = jnp.zeros((4 * channels, atom_rows), jnp.float32)
    coefficients = build_coefficients(summed, wave_vectors, filter_width)

    def backward(turn_index, running):
        k_piece = lax.dynamic_slice_in_dim(wave_vectors, turn_index * k_block, k_block, 1)
        coefficient_piece = lax.dynamic_slice_in_dim(coefficients, turn_index * k_block, k_block, 2)
        return running + project(coefficient_piece, k_piece, positions)

    fields = lax.fori_loop(0, k_turns, backward, empty_fields)
    fields = fields * (1.0 / math.sqrt(atom_rows * devices))
    pieces = [features]
    for direction, stride in ((0, 1), (1, -1)):
        chosen = jnp.take(features, send_along_x[direction], axis=0)
        pieces.append(passed_along(chosen, "gx", stride))
    first_table = jnp.concatenate(pieces, axis=0)
    pieces = [first_table]
    for direction, stride in ((0, 1), (1, -1)):
        chosen = jnp.take(first_table, send_along_y[direction], axis=0)
        pieces.append(passed_along(chosen, "gy", stride))
    ghost_table = jnp.concatenate(pieces, axis=0)
    radial_count = w_filter_in.shape[0]
    slot_total = neighbours.shape[0]
    slot_block = math.gcd(slot_total, 16)
    centers = 5.0 * jnp.arange(radial_count, dtype=jnp.float32) / (radial_count - 1)
    sharpness = 0.02 * (radial_count - 1) * (radial_count - 1)

    def add_slots(turn_index, running):
        first_slot = turn_index * slot_block
        neighbour_ids = lax.dynamic_slice_in_dim(neighbours, first_slot, slot_block, 0)
        lengths = lax.dynamic_slice_in_dim(distances, first_slot, slot_block, 0)
        offsets = lengths[..., None] - centers
        radial_basis = jnp.exp(-sharpness * offsets * offsets).astype(jnp.bfloat16)
        hidden_features = shifted_softplus(
            jnp.einsum("sar,rf->saf", radial_basis, w_filter_in, preferred_element_type=jnp.float32)
        ).astype(jnp.bfloat16)
        filter_values = jnp.einsum(
            "saf,fg->sag", hidden_features, filter_output_weight, preferred_element_type=jnp.float32
        )
        neighbour_rows = jnp.take(ghost_table, neighbour_ids, axis=0)
        slot_ids = first_slot + lax.broadcasted_iota(jnp.int32, neighbour_ids.shape, 0)
        envelope = jnp.where(
            slot_ids < neighbour_count[None, :], 0.5 * (jnp.cos(math.pi * lengths / 5.0) + 1.0), 0.0
        )
        return running + jnp.sum(
            envelope[..., None] * neighbour_rows.astype(jnp.float32) * filter_values, axis=0
        )

    messages = lax.fori_loop(
        0,
        slot_total // slot_block,
        add_slots,
        jnp.zeros((atom_rows, features.shape[1]), jnp.float32),
    )
    messages = messages.astype(jnp.bfloat16)
    updated = features.astype(jnp.float32) + jnp.dot(
        messages, update_weight, preferred_element_type=jnp.float32
    )
    updated = updated + jnp.dot(fields[:channels].T, w_long, precision=lax.Precision.HIGHEST)
    centred = charges.astype(jnp.float32) - mean_charge[:, None]
    field_parts = fields[channels:].reshape(3, channels, atom_rows)
    forces = -force_unit * jnp.sum(centred[None] * field_parts, axis=1)
    return (updated.astype(jnp.bfloat16), forces)


def solution(mesh):
    placed = (
        P(("gx", "gy"), None),
        P(None, ("gx", "gy")),
        P(),
        P(),
        P(),
        P(),
        P(),
        P(),
        P(),
        P(None, ("gx", "gy")),
        P(None, ("gx", "gy")),
        P(None, ("gx", "gy")),
        P(("gx", "gy")),
        P(None, ("gx", "gy")),
    )
    return jax.shard_map(
        per_device,
        mesh=mesh,
        in_specs=placed,
        out_specs=(P(("gx", "gy"), None), P(None, ("gx", "gy"))),
        check_vma=False,
    )
```

profile of v0, /device:TPU:1, one launch (start us, length us, event | category | flops | bytes accessed | tf_op | source)
XLA Modules:
  0.0 715.2 jit_solution(11780034854152128563)
XLA Ops:
  7.2 0.8 compare_and_fusion.3
  8.0 1.3 gather_fusion.1
  9.4 6.0 collective-permute-start
  15.5 1.3 gather_fusion.2
  16.9 4.7 collective-permute-start.1
  21.6 1.0 convert_reduce_fusion
  22.8 52.9 %while.43 = (s32[]{:T(128)}, f32[17,2,16384]{2,0,1:T(8,128)S(1)}, s32[3,16384]{1,0:T(4,128)}, f32[3,128]{1,0:T(4,128)}, bf16[17,128]{1,0:T(8,128)(2,1)S(1)}, /*index=5*/s32[]{:T(128)}, s32[]{:T(128)}, s32[]{:T(128)}, s32[]{:T(128)}) while((s32[]{:T(128)}, f32[17,2,16384]{2,0,1:T(8,128)S(1)}, s32[3,16384]{1,0:T(4,128)}, f32[3,128]{1,0:T(4,128)}, ...), condition=%wide.region_4.7_spmd, body=%wide.region_3.6_spmd.sunk | while | flops 20453380 | bytes 2624155 | solution.py:97
  22.8 0.8 slice_bitcast_fusion.8
  23.6 0.8 dynamic-slice_convert_fusion.4
  24.4 4.4 cosine_convert_fusion.4
  29.4 0.8 slice_bitcast_fusion.8
  31.0 4.4 cosine_convert_fusion.4
  36.0 0.8 slice_bitcast_fusion.8
  36.9 0.8 dynamic-slice_convert_fusion.4
  37.6 4.4 cosine_convert_fusion.4
  42.7 0.8 slice_bitcast_fusion.8
  44.3 4.4 cosine_convert_fusion.4
  49.3 0.8 slice_bitcast_fusion.8
  50.9 4.4 cosine_convert_fusion.4
  55.9 0.8 slice_bitcast_fusion.8
  57.5 4.4 cosine_convert_fusion.4
  62.5 0.8 slice_bitcast_fusion.8
  63.3 0.8 dynamic-slice_convert_fusion.4
  64.1 4.4 cosine_convert_fusion.4
  69.1 0.8 slice_bitcast_fusion.8
  70.7 4.4 cosine_convert_fusion.4
  76.6 106.4 %psum.14 = f32[16]{0:T(128)S(1)} all-reduce(f32[16]{0:T(128)S(1)} %get-tuple-element.555), channel_id=1, replica_groups=mesh['gx'=16,'gy'=32] {'gx','gy'}, use_global_device_ids=true, to_apply=%region_6.9 | all-reduce | flops 16 | bytes 128 | tf_op jit(solution)/shard_map/psum | solution.py:83
  183.5 2.5 multiply_subtract_fusion
  189.7 2.0 collective-permute-start.2
  192.4 5.4 collective-permute-start.3
  198.6 34.6 %while.44 = (s32[]{:T(128)}, f32[128,128]{1,0:T(8,128)S(1)}, s32[128]{0:T(128)S(1)}, f32[64,128]{1,0:T(8,128)}, s32[64,128]{1,0:T(8,128)S(1)}, /*index=5*/bf16[2...) while((s32[]{:T(128)}, f32[128,128]{1,0:T(8,128)S(1)}, ...), condition=%wide.region_2.5_spmd.clone, body=%wide.region_0.4_spmd.clone.sunk | while | flops 83294248 | bytes 4114405 | solution.py:147
  198.6 6.2 gather_fusion
  204.8 0.8 multiply_select_fusion.2
  206.0 1.1 fusion.64
  207.3 6.2 gather_fusion
  213.5 0.8 multiply_select_fusion.2
  214.7 1.1 fusion.64
  215.9 6.2 gather_fusion
  222.1 0.8 multiply_select_fusion.2
  223.3 1.1 fusion.64
  224.5 6.2 gather_fusion
  230.7 0.8 multiply_select_fusion.2
  232.0 1.1 fusion.64
  233.3 421.9 %all-reduce.3.cloned.1.call-done = f32[16,2,16384]{2,0,1:T(8,128)} async-done(((f32[16,2,16384]{2,0,1:T(8,128)}), f32[16,2,16384]{2,0,1:T(8,128)}) %all-reduce.3.cloned.1.call-update) | async-done | bytes 2097168 | tf_op jit(solution)/shard_map/psum | solution.py:99
  655.2 1.8 fusion.39
  657.5 2.5 maximum_maximum_fusion
  660.0 46.7 %while.45 = (s32[]{:T(128)}, f32[64,128]{1,0:T(8,128)S(1)}, bf16[64,2,16384]{2,0,1:T(8,128)(2,1)}, s32[3,16384]{1,0:T(4,128)S(1)}, f32[3,128]{1,0:T(4,128)S(1)},...) while((s32[]{:T(128)}, f32[64,128]{1,0:T(8,128)S(1)}, bf16[64,2,16384]{2,0,1:T(8,128)(2,1)}, ...), condition=%wide.region_9.12_spmd.clone, body=%wide.region_8.0_spmd.clone.sunk | while | flops 69752840 | bytes 2814629 | solution.py:108
  660.1 4.4 cosine_convert_fusion.5
  664.5 1.4 fusion.68
  666.0 4.4 cosine_convert_fusion.5
  670.3 1.4 fusion.68
  671.8 4.4 cosine_convert_fusion.5
  676.2 1.4 fusion.68
  677.6 4.4 cosine_convert_fusion.5
  682.0 1.4 fusion.68
  683.5 4.4 cosine_convert_fusion.5
  687.9 1.4 fusion.68
  689.3 4.4 cosine_convert_fusion.5
  693.7 1.4 fusion.68
  695.2 4.4 cosine_convert_fusion.5
  699.5 1.4 fusion.68
  701.0 4.4 cosine_convert_fusion.5
  705.4 1.4 fusion.68
  707.4 0.9 fusion.31
  (129 shorter events, 19.5 us)
Async XLA Ops:
  7.2 226.0 %copy-start = (bf16[128,128]{1,0:T(8,128)(2,1)S(1)}, bf16[128,128]{1,0:T(8,128)(2,1)}, u32[]{:S(2)}) copy-start(bf16[128,128]{1,0:T(8,128)(2,1)} %param.31) | copy-start | bytes 98308
  7.2 648.0 %all-reduce.3.cloned.1.call-start = ((), (), s32[]{:S(2)}) async-start(), calls=%async_computation | async-start | bytes 4194304 | tf_op jit(solution)/shard_map/psum | solution.py:99
  9.4 179.6 %collective-permute-start = (bf16[32,128]{1,0:T(8,128)(2,1)S(1)}, bf16[32,128]{1,0:T(8,128)(2,1)S(1)}, u32[]{:S(2)}, u32[]{:S(2)}) collective-permute-start(bf16[32,128]{1,0:T(8,128)(2,1)S(1)} %broadcast_select_fusion.3), channel_id=1, source_target_pairs={{480,0},{0,32},{32,64},{64,96},{96,128},{128,160},{160,192},{192,2... | collective-permute-start | bytes 24584 | tf_op jit(solution)/shard_map/ppermute | solution.py:15
  16.9 172.1 %collective-permute-start.1 = (bf16[32,128]{1,0:T(8,128)(2,1)S(1)}, bf16[32,128]{1,0:T(8,128)(2,1)S(1)}, u32[]{:S(2)}, u32[]{:S(2)}) collective-permute-start(bf16[32,128]{1,0:T(8,128)(2,1)S(1)} %broadcast_select_fusion.2), channel_id=1, source_target_pairs={{32,0},{64,32},{96,64},{128,96},{160,128},{192,160},{224,192},{256... | collective-permute-start | bytes 24584 | tf_op jit(solution)/shard_map/ppermute | solution.py:15
  75.7 110.3 %copy-start.1 = (bf16[128,128]{1,0:T(8,128)(2,1)S(1)}, bf16[128,128]{1,0:T(8,128)(2,1)}, u32[]{:S(2)}) copy-start(bf16[128,128]{1,0:T(8,128)(2,1)} %param.24) | copy-start | bytes 98308
  75.7 110.3 %copy-start.2 = (s32[3,16384]{1,0:T(4,128)S(1)}, s32[3,16384]{1,0:T(4,128)}, u32[]{:S(2)}) copy-start(s32[3,16384]{1,0:T(4,128)} %get-tuple-element.802) | copy-start | bytes 589828
  183.0 0.5 copy-start.8
  183.5 15.1 %copy-start.3 = (s32[64,128]{1,0:T(8,128)S(1)}, s32[64,128]{1,0:T(8,128)}, u32[]{:S(2)}) copy-start(s32[64,128]{1,0:T(8,128)} %param.35) | copy-start | bytes 98308
  183.5 15.1 %copy-start.4 = (bf16[20,128]{1,0:T(8,128)(2,1)S(1)}, bf16[20,128]{1,0:T(8,128)(2,1)}, u32[]{:S(2)}) copy-start(bf16[20,128]{1,0:T(8,128)(2,1)} %param.29) | copy-start | bytes 15364
  183.5 15.1 %copy-start.6 = (s32[128]{0:T(128)S(1)}, s32[128]{0:T(128)}, u32[]{:S(2)}) copy-start(s32[128]{0:T(128)} %param.36) | copy-start | bytes 1540
  186.0 12.6 %copy-start.9 = (bf16[128,128]{1,0:T(8,128)(2,1)S(1)}, bf16[128,128]{1,0:T(8,128)(2,1)}, u32[]{:S(2)}) copy-start(bf16[128,128]{1,0:T(8,128)(2,1)} %param.30) | copy-start | bytes 98308
  189.7 8.1 %collective-permute-start.2 = (bf16[32,128]{1,0:T(8,128)(2,1)S(1)}, bf16[32,128]{1,0:T(8,128)(2,1)S(1)}, u32[]{:S(2)}, u32[]{:S(2)}) collective-permute-start(bf16[32,128]{1,0:T(8,128)(2,1)S(1)} %broadcast_select_fusion.1), channel_id=1, source_target_pairs={{31,0},{0,1},{1,2},{2,3},{3,4},{4,5},{5,6},{6,7},{7,8},{8,9},{9,10... | collective-permute-start | bytes 24584 | tf_op jit(solution)/shard_map/ppermute | solution.py:15
  192.4 6.2 collective-permute-start.3
  657.5 2.5 copy-start.5
  660.0 47.4 %copy-start.7 = (f32[16,128]{1,0:T(8,128)S(1)}, f32[16,128]{1,0:T(8,128)}, u32[]{:S(2)}) copy-start(f32[16,128]{1,0:T(8,128)} %param.32) | copy-start | bytes 24580
Sparse Core Ops, SparseCore 0:
  186.2 469.0 all-reduce.2
where the time goes:
time: 717 us; the launch traced here: 715 us
  waiting for transfers between devices  423 us (59%)
  blocking collectives  106 us (15%)
  other arithmetic  91.1 us (13%)
  local copies, waits for them, and re-layouts  37.1 us (5%)
  matrix products  24.6 us (3%)
  starting transfers between devices  18.1 us (3%)
  between operations  14.3 us (2%)
    psum x1, waiting for transfers between devices, per_device(): summed = lax.psum(terms, ('gx', 'gy'))  422 us
    psum x1, blocking collectives, per_device(): lax.psum(jnp.sum(charges.astype(jnp.float32), axis=1), ('gx', 'gy'))  106 us
    another operation x18, other arithmetic  72 us
    gather x4, local copies, waits for them, and re-layouts, add_slots(): neighbour_rows = jnp.take(ghost_table, neighbour_ids, axis=0)  24.7 us
    ppermute x4, starting transfers between devices, passed_along(): return lax.ppermute(block, axis, route)  18.1 us
  transfers between devices with their start and end apart: 5, of which 2 were waited for; matrix products, arithmetic and copies ran while one was open for 14% of the time, Pallas kernels for 0%

commit v1 on v0

v1 whole, which is shorter than its diff:
```python
import functools
import math

import jax
import jax.numpy as jnp
from jax import lax
from jax.experimental import pallas as pl
from jax.experimental.pallas import tpu as pltpu
from jax.sharding import PartitionSpec as P

f32 = jnp.float32
bf16 = jnp.bfloat16

GX = 16
GY = 32
XY = 16
NZ = 16
ATOMS = 128
C = 16
K = 16384
PIECE = 512
PIECES = K // PIECE
TILES = 8
SLOTS = 64
RAW = 24
GROUP = 4
LAG = 4

TWO_PI = 2.0 * math.pi
FORCE_UNIT = 0.001
MAGIC = 12582912.0

SIN_POLY = (-0.79116057, 3.59775961, -7.30781532, 4.44287955)
COS_POLY = (-1.72807912, 5.7151373, -6.97763258, 1.41420395)


def horner(u, poly):
    value = poly[0] * u + poly[1]
    for term in poly[2:]:
        value = value * u + term
    return value


def cos_sin_turns(turns):
    r = turns - ((turns + MAGIC) - MAGIC)
    u = r * r
    s = r * horner(u, SIN_POLY)
    c = horner(u, COS_POLY)
    return 1.0 - s * s, s * c


def dot(a, b, **kw):
    return jnp.dot(a, b, preferred_element_type=f32, **kw)


def dot_nt(a, b):
    return lax.dot_general(a, b, (((1,), (1,)), ((), ())), preferred_element_type=f32)


def kernel(
    feat, pos, wv, fw, wch, win, wout, wup, wlong, sx, sy, nbr, cnt, dist,
    upd_o, frc_o,
    W, CS, CR, XS, XR, ZS, ZR, FALL, QS, QA, QB, QC, TAB, GS,
    scr, scr2, xt_s, qe_s, qf_s, mean_s, env_s, own_s, wgt_s, gt_s, wint_s, woutt_s,
    qa_s, qa_r, qb_s, qb_r, qc_s, qc_r, g_s, g_r, c_s, c_r, x_s, x_r, z_s, z_r, f_s, f_r,
    a_s, a_r, b_s, b_r,
):
    gx = lax.axis_index("gx")
    gy = lax.axis_index("gy")
    h = lax.rem(gx, 2)
    z = gy // 2
    m = (gx // 4) * 4 + lax.rem(gx // 2, 2) * 2 + lax.rem(gy, 2)

    def xy_dev(i):
        return ((i // 4) * 4 + lax.rem(i // 2, 2) * 2 + h, z * 2 + lax.rem(i, 2))

    def z_dev(i):
        return (gx, i * 2 + lax.rem(gy, 2))

    sib = (gx + 1 - 2 * h, gy)

    def wrap(i):
        return lax.rem(i + 2 * XY, XY)

    x_up = (lax.rem(gx + 1, GX), gy)
    x_down = (lax.rem(gx + GX - 1, GX), gy)
    y_up = (gx, lax.rem(gy + 1, GY))
    y_down = (gx, lax.rem(gy + GY - 1, GY))

    def rcopy(src, dst, ssem, rsem, dev):
        return pltpu.make_async_remote_copy(
            src_ref=src, dst_ref=dst, send_sem=ssem, recv_sem=rsem,
            device_id=dev, device_id_type=pl.DeviceIdType.MESH,
        )

    barrier = pltpu.get_barrier_semaphore()

    def greet(dev):
        pl.semaphore_signal(barrier, inc=1, device_id=dev, device_id_type=pl.DeviceIdType.MESH)

    def greet_ring(i, carry):
        greet(xy_dev(wrap(m + i)))
        greet(z_dev(wrap(z + i)))
        return carry

    greet(sib)
    for dev in (x_up, x_down, y_up, y_down):
        greet(dev)
    lax.fori_loop(1, XY, greet_ring, 0)

    features = feat[...]
    scr[...] = jnp.zeros_like(scr)
    scr[:, 0:C] = wch[...].astype(f32)
    charges = dot(features, scr[...].astype(bf16)).astype(bf16).astype(f32)
    charges_t = charges.T
    row_id = lax.broadcasted_iota(jnp.int32, (32, ATOMS), 0)
    qf_s[...] = charges_t[0:C]
    qe_s[...] = jnp.where(row_id == C, 1.0, charges_t[0:32]).astype(bf16)
    QS[0] = jnp.broadcast_to(jnp.sum(charges_t[0:C], axis=1, keepdims=True), (C, 128))

    x3 = pos[...]
    xhi = x3.astype(bf16).astype(f32)
    xmid = (x3 - xhi).astype(bf16).astype(f32)
    xlo = (x3 - xhi) - xmid
    scr[...] = jnp.zeros_like(scr)
    scr[0:3, :] = xhi
    scr[8:11, :] = xmid
    scr[16:19, :] = xlo
    xt_s[...] = scr[...].T.astype(bf16)

    lane_iota = lax.broadcasted_iota(jnp.int32, (ATOMS, 32), 0)

    def pick(list_ref, d, base):
        scr[:, 0:32] = jnp.where(list_ref[d : d + 1, :] == lane_iota + base, 1.0, 0.0)
        return scr[...].T[0:32].astype(bf16)

    scr[...] = jnp.zeros_like(scr)
    TAB[0:ATOMS] = features
    for d in range(2):
        GS[d] = dot(pick(sx, d, 0), features).astype(bf16)

    pl.semaphore_wait(barrier, 5 + 2 * (XY - 1))

    ghost = [
        rcopy(GS.at[0], TAB.at[pl.ds(128, 32)], g_s.at[0], g_r.at[0], x_up),
        rcopy(GS.at[1], TAB.at[pl.ds(160, 32)], g_s.at[1], g_r.at[1], x_down),
        rcopy(GS.at[2], TAB.at[pl.ds(192, 32)], g_s.at[2], g_r.at[2], y_up),
        rcopy(GS.at[3], TAB.at[pl.ds(224, 32)], g_s.at[3], g_r.at[3], y_down),
    ]

    def qa_copy(i, slot):
        return rcopy(QS.at[0], QA.at[slot], qa_s.at[i], qa_r.at[slot], xy_dev(i))

    def qb_copy(i, slot):
        return rcopy(QS.at[1], QB.at[slot], qb_s.at[i], qb_r.at[slot], z_dev(i))

    qc_copy = rcopy(QS.at[2], QC, qc_s, qc_r, sib)

    def start_qa(i, carry):
        qa_copy(wrap(m + i), m).start()
        return carry

    lax.fori_loop(1, XY, start_qa, 0)
    ghost[0].start()
    ghost[1].start()

    def reduce_qa():
        def wait(i, carry):
            j = wrap(m - i)
            qa_copy(j, j).wait_recv()
            return carry

        lax.fori_loop(1, XY, wait, 0)
        QA[m] = QS[0]
        total = QA[0]
        for j in range(1, XY):
            total = total + QA[j]
        QS[1] = total

        def start(i, carry):
            qb_copy(wrap(z + i), z).start()
            return carry

        lax.fori_loop(1, NZ, start, 0)

    def reduce_qb():
        def wait(i, carry):
            j = wrap(z - i)
            qb_copy(j, j).wait_recv()
            return carry

        lax.fori_loop(1, NZ, wait, 0)
        QB[z] = QS[1]
        total = QB[0]
        for j in range(1, NZ):
            total = total + QB[j]
        QS[2] = total
        qc_copy.start()

    def reduce_qc():
        qc_copy.wait_recv()
        mean = (QS[2] + QC[...]) * (1.0 / (GX * GY * ATOMS))
        mean_s[...] = jnp.concatenate([mean] * (PIECE // 128), axis=1)

    def wave_piece(g):
        k3 = wv[:, pl.ds(pl.multiple_of(g * PIECE, PIECE), PIECE)].astype(f32)
        k8 = jnp.concatenate([k3, jnp.zeros((5, PIECE), f32)], axis=0)
        kb = jnp.concatenate([k8, k8, k8, jnp.zeros((8, PIECE), f32)], axis=0).astype(bf16)
        xt = xt_s[:, 0:32]
        qe = qe_s[...]
        raws = ([], [])
        for j in range(PIECE // 128):
            lanes = slice(j * 128, (j + 1) * 128)
            cos, sin = cos_sin_turns(dot(xt, kb[:, lanes]))
            for p, wave in enumerate((cos.astype(bf16), sin.astype(bf16))):
                W[g, p, :, lanes] = wave
                raws[p].append(dot(qe, wave))
        return [jnp.concatenate(raw, axis=1)[0:RAW] for raw in raws]

    def core_copy(i):
        return rcopy(CS.at[i], CR.at[i], c_s.at[i], c_r.at[i], sib)

    def other_half(s, carry):
        i = wrap(m + s)
        raw = wave_piece((1 - h) * XY + i)
        CS[i, 0] = raw[0]
        CS[i, 1] = raw[1]
        core_copy(i).start()
        return carry

    def xy_copy(i, slot):
        return rcopy(XS.at[i], XR.at[slot], x_s.at[i], x_r.at[slot], xy_dev(i))

    def own_terms(s):
        i = wrap(m + s)
        raw = wave_piece(h * XY + i)
        core_copy(i).wait_recv()
        mean = mean_s[...]
        terms = []
        for p in range(2):
            total = raw[p] + CR[i, p]
            terms.append(total[0:C] - mean * total[C : C + 1])
        return i, terms

    def own_half(s, carry):
        i, terms = own_terms(s)
        XS[i, 0:C] = terms[0].astype(bf16)
        XS[i, C : 2 * C] = terms[1].astype(bf16)
        xy_copy(i, m).start()
        return carry

    lax.fori_loop(1, 6, other_half, 0)
    reduce_qa()
    ghost[0].wait_recv()
    ghost[1].wait_recv()
    scr[...] = jnp.zeros_like(scr)
    for d in range(2):
        rows = dot(pick(sy, d, 0), TAB[0:128]) + dot(pick(sy, d, 128)[:, 0:64], TAB[128:192])
        GS[2 + d] = rows.astype(bf16)
    ghost[2].start()
    ghost[3].start()
    lax.fori_loop(6, 12, other_half, 0)
    reduce_qb()
    lax.fori_loop(12, 17, other_half, 0)
    reduce_qc()
    lax.fori_loop(1, XY, own_half, 0)
    i_own, terms = own_terms(0)
    XR[m, 0:C] = terms[0].astype(bf16)
    XR[m, C : 2 * C] = terms[1].astype(bf16)

    scr[...] = jnp.zeros_like(scr)
    scr[0:20, :] = win[...].astype(f32)
    wint_s[...] = scr[...].T.astype(bf16)
    woutt_s[...] = wout[...].astype(f32).T.astype(bf16)
    ghost[2].wait_recv()
    ghost[3].wait_recv()
    gt_s[:, 0:128] = TAB[0:128].astype(f32).T.astype(bf16)
    gt_s[:, 128:256] = TAB[128:256].astype(f32).T.astype(bf16)
    slot_id = lax.broadcasted_iota(jnp.int32, (SLOTS, ATOMS), 0)
    swing, _ = cos_sin_turns(dist[...] * 0.1)
    env_s[...] = jnp.where(slot_id < cnt[...], 0.5 * (swing + 1.0), 0.0)

    centre = lax.broadcasted_iota(jnp.int32, (32, ATOMS), 0).astype(f32) * (5.0 / 19.0)
    table_row = lax.broadcasted_iota(jnp.int32, (2 * ATOMS, ATOMS), 0)
    sharpness = 0.02 * 19.0 * 19.0

    def message_step(i, running):
        base = i * GROUP
        basis, hot = [], []
        for u in range(GROUP):
            offset = dist[pl.ds(base + u, 1), :] - centre
            basis.append(jnp.exp(-sharpness * offset * offset).astype(bf16))
            hot.append(jnp.where(nbr[pl.ds(base + u, 1), :] == table_row, 1.0, 0.0).astype(bf16))
        for u in range(0, GROUP, 2):
            pre = dot(wint_s[:, 0:32], jnp.concatenate(basis[u : u + 2], axis=1))
            hidden = jnp.log(0.5 * jnp.exp(pre) + 0.5).astype(bf16)
            filters = dot(woutt_s[...], hidden)
            rows = dot(gt_s[...], jnp.concatenate(hot[u : u + 2], axis=1))
            both = filters * rows
            running = (
                running
                + env_s[pl.ds(base + u, 1), :] * both[:, 0:128]
                + env_s[pl.ds(base + u + 1, 1), :] * both[:, 128:256]
            )
        return running

    steps = SLOTS // GROUP
    messages = lax.fori_loop(0, steps // 2, message_step, jnp.zeros((128, ATOMS), f32))

    def wait_xy(i, carry):
        j = wrap(m - i)
        xy_copy(j, j).wait_recv()
        return carry

    lax.fori_loop(1, XY, wait_xy, 0)
    for kb in range(4):
        lanes = slice(kb * 128, (kb + 1) * 128)
        for p in range(2):
            rows = slice(p * C, (p + 1) * C)
            total = XR[0, rows, lanes].astype(f32)
            for j in range(1, XY):
                total = total + XR[j, rows, lanes].astype(f32)
            ZS[2 * kb + p] = total.astype(bf16)

    def z_copy(i, slot):
        return rcopy(ZS.at[lax.rem(i, TILES)], ZR.at[slot], z_s.at[i], z_r.at[slot], z_dev(i))

    def start_z(i, carry):
        z_copy(wrap(z + i), z).start()
        return carry

    lax.fori_loop(1, NZ, start_z, 0)
    tile = lax.rem(z, TILES)
    ZR[z] = ZS[tile]

    g_own = h * XY + m
    k_tile = pl.multiple_of(g_own * PIECE + (tile // 2) * 128, 128)
    kt = wv[:, pl.ds(k_tile, 128)].astype(f32)
    q2 = (TWO_PI * TWO_PI) * (
        kt[0:1] * kt[0:1] + kt[1:2] * kt[1:2] + 0.25 * (kt[2:3] * kt[2:3])
    )
    eye = lax.broadcasted_iota(jnp.int32, (C, C), 0) == lax.broadcasted_iota(jnp.int32, (C, C), 1)
    width = jnp.sum(jnp.where(eye, jnp.broadcast_to(fw[...], (C, C)), 0.0), axis=1, keepdims=True)
    weight = jnp.exp(-0.5 * (width * width) * q2) * ((TWO_PI * TWO_PI) / q2)
    wgt_s[...] = weight

    messages = lax.fori_loop(steps // 2, (3 * steps) // 4, message_step, messages)

    def wait_z(i, carry):
        j = wrap(z - i)
        z_copy(j, j).wait_recv()
        return carry

    lax.fori_loop(1, NZ, wait_z, 0)
    total = ZR[0].astype(f32)
    for j in range(1, NZ):
        total = total + ZR[j].astype(f32)
    FALL[g_own, tile] = (total * wgt_s[...]).astype(bf16)

    def f_copy(delta, slot_tile, slot):
        return rcopy(
            FALL.at[g_own, slot_tile], FALL.at[g_own, slot_tile], f_s.at[slot], f_r.at[slot_tile],
            z_dev(wrap(z + delta)),
        )

    for n, delta in enumerate((1, -1, 2, -2, 3, -3, 4)):
        f_copy(delta, tile, n).start()
    messages = lax.fori_loop((3 * steps) // 4, steps, message_step, messages)

    def wait_f(i, carry):
        f_copy(1, lax.rem(tile + i, TILES), 0).wait_recv()
        return carry

    lax.fori_loop(1, TILES, wait_f, 0)

    def a_copy(i, slot):
        return rcopy(
            FALL.at[h * XY + slot], FALL.at[h * XY + slot], a_s.at[i], a_r.at[slot], xy_dev(i)
        )

    def b_copy(half, i):
        return rcopy(FALL.at[half * XY + i], FALL.at[half * XY + i], b_s.at[i], b_r.at[i], sib)

    b_copy(h, m).start()

    def start_a(i, carry):
        a_copy(wrap(m + i), m).start()
        return carry

    lax.fori_loop(1, XY, start_a, 0)

    def project(g, running):
        kf = wv[:, pl.ds(pl.multiple_of(g * PIECE, PIECE), PIECE)].astype(f32) * TWO_PI
        f0 = jnp.concatenate([FALL[g, 2 * kb] for kb in range(4)], axis=1)
        f1 = jnp.concatenate([FALL[g, 2 * kb + 1] for kb in range(4)], axis=1)
        f0w, f1w = f0.astype(f32), f1.astype(f32)
        first, second = [f0], [f1]
        for d in range(3):
            first.append((kf[d : d + 1] * f1w).astype(bf16))
            second.append((-kf[d : d + 1] * f0w).astype(bf16))
        running = running + dot_nt(jnp.concatenate(first, axis=0), W[g, 0])
        return running + dot_nt(jnp.concatenate(second, axis=0), W[g, 1])

    def near(i, running):
        j = wrap(m - i)
        a_copy(j, j).wait_recv()
        b_copy(h, j).start()
        return project(h * XY + j, running)

    def far(i, running):
        j = wrap(m - i)
        b_copy(1 - h, j).wait_recv()
        return project((1 - h) * XY + j, running)

    fields = project(g_own, jnp.zeros((4 * C, ATOMS), f32))
    fields = lax.fori_loop(1, LAG, near, fields)
    fields = lax.fori_loop(LAG, XY, lambda i, v: far(i - LAG, near(i, v)), fields)
    fields = lax.fori_loop(XY - LAG, XY, far, fields)
    fields = fields * (1.0 / math.sqrt(GX * GY * ATOMS))

    centred = qf_s[...] - mean_s[:, 0:128]
    for d in range(3):
        part = fields[(d + 1) * C : (d + 2) * C]
        frc_o[d : d + 1, :] = -FORCE_UNIT * jnp.sum(centred * part, axis=0, keepdims=True)
    scr[...] = jnp.zeros_like(scr)
    scr[0:C, :] = fields[0:C]
    scr2[...] = jnp.zeros_like(scr2)
    scr2[0:C, :] = wlong[...]
    long_part = dot(scr[...].T, scr2[...], precision=lax.Precision.HIGHEST)
    message_rows = messages.astype(bf16).astype(f32).T.astype(bf16)
    updated = features.astype(f32) + dot(message_rows, wup[...])
    upd_o[...] = (updated + long_part).astype(bf16)

    qc_copy.wait_send()
    for copy in ghost:
        copy.wait_send()

    def drain(i, carry):
        jm = wrap(m + i)
        jz = wrap(z + i)
        qa_copy(jm, m).wait_send()
        qb_copy(jz, z).wait_send()
        xy_copy(jm, m).wait_send()
        z_copy(jz, z).wait_send()
        a_copy(jm, m).wait_send()
        return carry

    lax.fori_loop(1, XY, drain, 0)

    def drain_core(i, carry):
        core_copy(i).wait_send()
        b_copy(h, i).wait_send()
        return carry

    lax.fori_loop(0, XY, drain_core, 0)
    for n in range(TILES - 1):
        f_copy(1, tile, n).wait_send()


def per_device(*args):
    feat, pos, wv, fw, wch, win, wout, wup, wlong, sx, sy, nbr, cnt, dist = args
    dma = pltpu.SemaphoreType.DMA
    scratch = [
        pltpu.VMEM((PIECES, 2, ATOMS, PIECE), bf16),
        pltpu.VMEM((XY, 2, RAW, PIECE), f32),
        pltpu.VMEM((XY, 2, RAW, PIECE), f32),
        pltpu.VMEM((XY, 2 * C, PIECE), bf16),
        pltpu.VMEM((XY, 2 * C, PIECE), bf16),
        pltpu.VMEM((TILES, C, 128), bf16),
        pltpu.VMEM((NZ, C, 128), bf16),
        pltpu.VMEM((PIECES, TILES, C, 128), bf16),
        pltpu.VMEM((3, C, 128), f32),
        pltpu.VMEM((XY, C, 128), f32),
        pltpu.VMEM((NZ, C, 128), f32),
        pltpu.VMEM((C, 128), f32),
        pltpu.VMEM((2 * ATOMS, 128), bf16),
        pltpu.VMEM((4, 32, 128), bf16),
        pltpu.VMEM((128, 128), f32),
        pltpu.VMEM((128, 128), f32),
        pltpu.VMEM((128, 128), bf16),
        pltpu.VMEM((32, ATOMS), bf16),
        pltpu.VMEM((C, ATOMS), f32),
        pltpu.VMEM((C, PIECE), f32),
        pltpu.VMEM((SLOTS, ATOMS), f32),
        pltpu.VMEM((8, 128), f32),
        pltpu.VMEM((C, 128), f32),
        pltpu.VMEM((128, 256), bf16),
        pltpu.VMEM((128, 128), bf16),
        pltpu.VMEM((128, 128), bf16),
        dma((XY,)), dma((XY,)), dma((NZ,)), dma((NZ,)), dma, dma,
        dma((4,)), dma((4,)),
        dma((XY,)), dma((XY,)),
        dma((XY,)), dma((XY,)),
        dma((NZ,)), dma((NZ,)),
        dma((TILES,)), dma((TILES,)),
        dma((XY,)), dma((XY,)),
        dma((XY,)), dma((XY,)),
    ]
    vmem = pl.BlockSpec(memory_space=pltpu.VMEM)
    return pl.pallas_call(
        kernel,
        out_shape=(
            jax.ShapeDtypeStruct((ATOMS, 128), bf16),
            jax.ShapeDtypeStruct((3, ATOMS), f32),
        ),
        in_specs=[vmem] * 14,
        out_specs=(vmem, vmem),
        scratch_shapes=scratch,
        compiler_params=pltpu.CompilerParams(
            collective_id=0, has_side_effects=True, vmem_limit_bytes=48 * 1024 * 1024
        ),
    )(
        feat, pos, wv, fw.reshape(1, C), wch, win, wout, wup, wlong, sx, sy, nbr,
        cnt.reshape(1, ATOMS), dist,
    )


def solution(mesh):
    atoms_first = P(("gx", "gy"), None)
    atoms_last = P(None, ("gx", "gy"))
    placed = (
        atoms_first, atoms_last, P(), P(), P(), P(), P(), P(), P(),
        atoms_last, atoms_last, atoms_last, P(("gx", "gy")), atoms_last,
    )
    return jax.shard_map(
        per_device,
        mesh=mesh,
        in_specs=placed,
        out_specs=(atoms_first, atoms_last),
        check_vma=False,
    )
```

time: 717 us -> 94 us (0.13)
  waiting for transfers between devices: 423 us -> 0 us
  blocking collectives: 106 us -> 0 us
  other arithmetic: 91.1 us -> 0 us
  Pallas kernels: 0 us -> 84 us
  local copies, waits for them, and re-layouts: 37.1 us -> 8.72 us
  matrix products: 24.6 us -> 0 us
  starting transfers between devices: 18.1 us -> 0 us
  between operations: 14.3 us -> 0.71 us
    psum x1 -> x0, waiting for transfers between devices: 422 us -> none  [per_device(): summed = lax.psum(terms, ('gx', 'gy'))]
    psum x1 -> x0, blocking collectives: 106 us -> none  [per_device(): lax.psum(jnp.sum(charges.astype(jnp.float32), axis=1), ('gx', 'gy'))]
    pallas_call x0 -> x1, Pallas kernels: none -> 84 us  [per_device(): pl.pallas_call(kernel, out_shape=(jax.ShapeDtypeStruct((ATOMS, 128), bf16...]
    another operation x18 -> x0, other arithmetic: 72 us -> none
    gather x8 -> x0, local copies, waits for them, and re-layouts: 28.6 us -> none  [the longest x4 24.7 us: add_slots(): neighbour_rows = jnp.take(ghost_table, neighbour_ids, axis=0)]
    dot_general x27 -> x0, matrix products: 24.6 us -> none  [the longest x8 11.1 us: project(): jnp.einsum('rpk,pka->ra', coefficient_piece, wave_table, preferred_elemen...]
    ppermute x4 -> x0, starting transfers between devices: 18.1 us -> none  [passed_along(): return lax.ppermute(block, axis, route)]
    unnamed x24 -> x29, local copies, waits for them, and re-layouts: 1.34 us -> 8.72 us
  transfers between devices with their start and end apart: 5 -> 0, of which waited for: 2 -> 0; matrix products, arithmetic and copies ran while one was open for 14% -> 0% of each run, Pallas kernels for 0% -> 0%
where the time goes in v1:
time: 94 us; the launch traced here: 93.4 us
  Pallas kernels  84 us (89%)
  local copies, waits for them, and re-layouts  8.72 us (9%)
    pallas_call x1, Pallas kernels, per_device(): pl.pallas_call(kernel, out_shape=(jax.ShapeDtypeStruct((ATOMS, 128), bf16...  84 us
    unnamed x29, local copies, waits for them, and re-layouts  8.72 us

profile of v1, /device:TPU:1, one launch (start us, length us, event | category | flops | bytes accessed | tf_op | source)
XLA Modules:
  0.0 93.4 jit_solution(18038876983757017278)
XLA Ops:
  0.6 0.0 copy-start.1
  0.6 0.0 copy-start.7
  0.7 0.0 copy-start.9
  0.7 0.0 copy-start.11
  0.7 0.8 copy.16.wch
  1.5 0.0 copy-done.1
  1.5 0.0 copy-done.7
  1.5 0.0 copy-done.9
  1.5 0.0 copy-done.11
  1.5 0.0 copy-start
  1.5 0.9 %copy-done = s32[3,16384]{1,0:T(4,128)S(1)} copy-done((s32[3,16384]{1,0:T(4,128)S(1)}, s32[3,16384]{1,0:T(4,128)}, u32[]{:S(2)}) %copy-start) | copy-done | bytes 196632
  2.5 0.0 copy-start.2
  2.5 0.8 copy-done.2
  3.2 0.0 copy-start.3
  3.2 0.8 copy-done.3
  4.0 0.0 copy-start.4
  4.0 0.8 copy-done.4
  4.8 0.0 copy-start.5
  4.8 0.8 copy-done.5
  5.5 0.0 copy-start.6
  5.5 0.7 copy-done.6
  6.2 0.0 copy-start.8
  6.2 0.7 copy-done.8
  6.9 0.0 copy-start.10
  6.9 0.7 copy-done.10
  7.6 0.0 copy-start.12
  7.6 0.7 copy-done.12
  8.2 84.0 %shard_map.149 = (bf16[128,128]{1,0:T(8,128)(2,1)S(1)}, f32[3,128]{1,0:T(4,128)S(1)}) custom-call(bf16[128,128]{1,0:T(8,128)(2,1)S(1)} %copy-done.1, f32[3,128]{1,0:T(4,128)S(1)} %copy-done.8, s32[3,16384]{1,0:T(4,128)S(1)} %copy-done, f32[1,16]{1,0:T(1,128)S(1)} %bitcast.2, bf16[128,16]{1,0:T(8,128)(2,1)S(1)} %copy.16.wch, bf16[20,128]{1,0:T(8,128)(2,1)S(1)} %copy-done.7, ...), custom_call_target="tpu_custom_call" | custom-call | tf_op jit(solution)/shard_map/pallas_call | solution.py:500
  92.2 0.6 copy.19
  92.8 0.6 copy.20
Async XLA Ops:
  0.6 0.9 copy-start.1
  0.6 0.9 copy-start.7
  0.7 0.9 copy-start.9
  0.7 0.9 copy-start.11
  1.5 1.0 %copy-start = (s32[3,16384]{1,0:T(4,128)S(1)}, s32[3,16384]{1,0:T(4,128)}, u32[]{:S(2)}) copy-start(s32[3,16384]{1,0:T(4,128)} %wv.1) | copy-start | bytes 589828
  2.5 0.8 copy-start.2
  3.2 0.8 copy-start.3
  4.0 0.8 copy-start.4
  4.8 0.8 copy-start.5
  5.5 0.7 copy-start.6
  6.2 0.7 copy-start.8
  6.9 0.7 copy-start.10
  7.6 0.7 copy-start.12

commit v2 on v1

v2 whole, which is shorter than its diff:
```python
import functools
import math

import jax
import jax.numpy as jnp
from jax import lax
from jax.experimental import pallas as pl
from jax.experimental.pallas import tpu as pltpu
from jax.sharding import PartitionSpec as P

f32 = jnp.float32
bf16 = jnp.bfloat16

GX = 16
GY = 32
XY = 16
NZ = 16
ATOMS = 128
C = 16
K = 16384
PIECE = 512
PIECES = K // PIECE
TILES = 8
KBS = 4
SLOTS = 64
RAW = 24
GROUP = 8
LAG = 3

TWO_PI = 2.0 * math.pi
FORCE_UNIT = 0.001
MAGIC = 12582912.0

SIN_POLY = (-0.79116057, 3.59775961, -7.30781532, 4.44287955)
COS_POLY = (-1.72807912, 5.7151373, -6.97763258, 1.41420395)


def horner(u, poly):
    value = poly[0] * u + poly[1]
    for term in poly[2:]:
        value = value * u + term
    return value


def cos_sin_turns(turns):
    r = turns - ((turns + MAGIC) - MAGIC)
    u = r * r
    s = r * horner(u, SIN_POLY)
    c = horner(u, COS_POLY)
    return 1.0 - s * s, s * c


def dot(a, b, **kw):
    return jnp.dot(a, b, preferred_element_type=f32, **kw)


def dot_nt(a, b):
    return lax.dot_general(a, b, (((1,), (1,)), ((), ())), preferred_element_type=f32)


def kernel(*refs):
    sources, (upd_o, frc_o), held, rest = refs[:14], refs[14:16], refs[16:30], refs[30:]
    feat, pos, wv, fw, wch, win, wout, wup, wlong, sx, sy, nbr, cnt, dist = held
    (W, WA, WB, TA, TB, CS, CR, XS, XR, ZS, ZR, FALL, QS, QA, QB, QC, TAB, GS,
    scr, scr2, base_s, xt_s, qe_s, qf_s, mean_s, env_s, wgt_s, gt_s, wint_s, woutt_s,
    qa_s, qa_r, qb_s, qb_r, qc_s, qc_r, g_s, g_r, c_s, c_r, x_s, x_r, z_s, z_r, f_s, f_r,
    a_s, a_r, b_s, b_r, in_sem) = rest
    loads = [
        pltpu.make_async_copy(sources[n], held[n], in_sem.at[n]) for n in range(14)
    ]
    first_loads = (1, 2, 0, 4)
    later_loads = [n for n in range(14) if n not in first_loads]
    for n in first_loads:
        loads[n].start()
    gx = lax.axis_index("gx")
    gy = lax.axis_index("gy")
    h = lax.rem(gx, 2)
    z = gy // 2
    m = (gx // 4) * 4 + lax.rem(gx // 2, 2) * 2 + lax.rem(gy, 2)

    def xy_dev(i):
        return ((i // 4) * 4 + lax.rem(i // 2, 2) * 2 + h, z * 2 + lax.rem(i, 2))

    def z_dev(i):
        return (gx, i * 2 + lax.rem(gy, 2))

    sib = (gx + 1 - 2 * h, gy)

    def wrap(i):
        return lax.rem(i + 2 * XY, XY)

    def bend(a):
        return lax.rem(2 + a + a // 2 + 2 * (a // 3), 4)

    def xy_to(n):
        dy, dx = bend(n // 4), bend(lax.rem(n, 4))
        return lax.rem(m // 4 + dy, 4) * 4 + lax.rem(lax.rem(m, 4) + dx, 4)

    def xy_from(n):
        dy, dx = bend(n // 4), bend(lax.rem(n, 4))
        return lax.rem(m // 4 + 4 - dy, 4) * 4 + lax.rem(lax.rem(m, 4) + 4 - dx, 4)

    def far(n):
        odd = lax.rem(n, 2)
        return 8 + (1 - odd) * (n // 2) - odd * ((n + 1) // 2)

    def z_to(n):
        return lax.rem(z + far(n), NZ)

    def z_from(n):
        return lax.rem(z + NZ - far(n), NZ)

    x_up = (lax.rem(gx + 1, GX), gy)
    x_down = (lax.rem(gx + GX - 1, GX), gy)
    y_up = (gx, lax.rem(gy + 1, GY))
    y_down = (gx, lax.rem(gy + GY - 1, GY))

    def rcopy(src, dst, ssem, rsem, dev):
        return pltpu.make_async_remote_copy(
            src_ref=src, dst_ref=dst, send_sem=ssem, recv_sem=rsem,
            device_id=dev, device_id_type=pl.DeviceIdType.MESH,
        )

    barrier = pltpu.get_barrier_semaphore()

    def greet(dev):
        pl.semaphore_signal(barrier, inc=1, device_id=dev, device_id_type=pl.DeviceIdType.MESH)

    def greet_ring(i, carry):
        greet(z_dev(z_to(i)))
        greet(xy_dev(xy_to(i)))
        return carry

    lax.fori_loop(0, XY - 1, greet_ring, 0)
    greet(sib)
    for dev in (x_up, x_down, y_up, y_down):
        greet(dev)
    for n in later_loads:
        loads[n].start()

    loads[1].wait()
    x3 = pos[...]
    xhi = x3.astype(bf16).astype(f32)
    xmid = (x3 - xhi).astype(bf16).astype(f32)
    xlo = (x3 - xhi) - xmid
    scr2[...] = jnp.zeros_like(scr2)
    scr2[0:3, :] = xhi
    scr2[8:11, :] = xmid
    scr2[16:19, :] = xlo
    xt_s[...] = scr2[...].T.astype(bf16)
    for n in (2, 0, 4):
        loads[n].wait()
    features = feat[...]
    charges_t = dot_nt(wch[...], features).astype(bf16).astype(f32)
    row_id = lax.broadcasted_iota(jnp.int32, (32, ATOMS), 0)
    qf_s[...] = charges_t
    padded = jnp.concatenate([charges_t, jnp.zeros((C, ATOMS), f32)], axis=0)
    qe_s[...] = jnp.where(row_id == C, 1.0, padded).astype(bf16)
    own_sum = jnp.broadcast_to(jnp.sum(charges_t, axis=1, keepdims=True), (C, 128))
    QS[0] = own_sum
    mean_s[...] = jnp.concatenate([own_sum * (1.0 / ATOMS)] * KBS, axis=1)

    lane_iota = lax.broadcasted_iota(jnp.int32, (ATOMS, 32), 0)

    def pick(list_ref, d, base):
        scr[:, 0:32] = jnp.where(list_ref[d : d + 1, :] == lane_iota + base, 1.0, 0.0)
        return scr[...].T[0:32].astype(bf16)

    ghost = [
        rcopy(GS.at[0], TAB.at[pl.ds(128, 32)], g_s.at[0], g_r.at[0], x_up),
        rcopy(GS.at[1], TAB.at[pl.ds(160, 32)], g_s.at[1], g_r.at[1], x_down),
        rcopy(GS.at[2], TAB.at[pl.ds(192, 32)], g_s.at[2], g_r.at[2], y_up),
        rcopy(GS.at[3], TAB.at[pl.ds(224, 32)], g_s.at[3], g_r.at[3], y_down),
    ]

    def qa_copy(i, slot):
        return rcopy(QS.at[0], QA.at[slot], qa_s, qa_r, xy_dev(i))

    qa_all = rcopy(QA.at[pl.ds(0, XY - 1)], QA.at[pl.ds(0, XY - 1)], qa_s, qa_r, sib)
    qc_copy = rcopy(QS.at[1], QC, qc_s, qc_r, sib)

    def qb_copy(i, slot):
        return rcopy(QS.at[2], QB.at[slot], qb_s, qb_r, z_dev(i))

    qb_all = rcopy(QB.at[pl.ds(0, NZ - 1)], QB.at[pl.ds(0, NZ - 1)], qb_s, qb_r, sib)

    def start_qa(n, carry):
        qa_copy(xy_to(n), m).start()
        return carry

    def sum_plane():
        qa_all.wait_recv()
        QA[m] = QS[0]
        total = QA[0]
        for j in range(1, XY):
            total = total + QA[j]
        QS[1] = total
        qc_copy.start()

    def sum_cores():
        qc_copy.wait_recv()
        QS[2] = QS[1] + QC[...]

        def start(n, carry):
            qb_copy(z_to(n), z).start()
            return carry

        lax.fori_loop(0, NZ - 1, start, 0)

    def piece_of(n):
        half = jnp.where(n < XY, 1 - h, h)
        return half * XY + xy_to(lax.rem(n, XY))

    def phases(n, turns):
        first = pl.multiple_of(piece_of(n) * PIECE, PIECE)
        k3 = wv[:, pl.ds(first, PIECE)].astype(f32)
        k8 = jnp.concatenate([k3, jnp.zeros((5, PIECE), f32)], axis=0)
        kb = jnp.concatenate([k8, k8, k8, jnp.zeros((8, PIECE), f32)], axis=0).astype(bf16)
        turns[...] = dot(xt_s[:, 0:32], kb)

    def waves(n, turns, recent):
        g = piece_of(n)
        for j in range(PIECE // 128):
            lanes = slice(j * 128, (j + 1) * 128)
            for p, wave in enumerate(cos_sin_turns(turns[:, lanes])):
                wave = wave.astype(bf16)
                W[g, p, :, lanes] = wave
                recent[p, :, lanes] = wave

    def meet(recent):
        return [dot(qe_s[...], recent[p])[0:RAW] for p in range(2)]

    def core_copy(i):
        return rcopy(CS.at[i], CR.at[i], c_s, c_r.at[i], sib)

    core_all = rcopy(CS, CR, c_s, c_r.at[0], sib)

    def keep_core(n, raw):
        i = xy_to(n)
        CS[i, 0] = raw[0]
        CS[i, 1] = raw[1]

    def xy_copy(i, slot):
        return rcopy(XS.at[i], XR.at[slot], x_s, x_r, xy_dev(i))

    xy_all = rcopy(XR.at[pl.ds(0, XY - 1)], XR.at[pl.ds(0, XY - 1)], x_s, x_r, sib)

    def split_units(units):
        high = units.astype(bf16).astype(f32)
        return jnp.concatenate([high, units - high], axis=0)

    def put_terms(i, raw, keep):
        core_copy(i).wait_recv()
        offset = mean_s[...]
        units = []
        for p in range(2):
            total = raw[p] + CR[i, p]
            unit = total[C : C + 1]
            units.append(unit)
            terms = (total[0:C] - offset * unit).astype(bf16)
            for kb in range(KBS):
                keep[2 * kb + p] = terms[:, kb * 128 : (kb + 1) * 128]
        split = split_units(jnp.concatenate(units, axis=0))
        keep[TILES] = jnp.concatenate(
            [split[:, kb * 128 : (kb + 1) * 128] for kb in range(KBS)], axis=0
        ).astype(bf16)

    def send_xy(n, raw):
        i = xy_to(lax.rem(n, XY))
        put_terms(i, raw, XS.at[i])
        xy_copy(i, m).start()

    def two_pieces(use):
        def body(step, carry):
            n = 2 * step + 1
            phases(n + 1, TA)
            raw = meet(WA)
            waves(n, TB, WB)
            use(n - 1, raw)
            phases(n + 2, TB)
            raw = meet(WB)
            waves(n + 1, TA, WA)
            use(n, raw)
            return carry

        return body

    phases(0, TA)
    phases(1, TB)
    waves(0, TA, WA)
    lax.fori_loop(0, 8, two_pieces(keep_core), 0)

    pl.semaphore_wait(barrier, 5 + 2 * (XY - 1))

    def start_core(n, carry):
        core_copy(xy_to(n)).start()
        return carry

    lax.fori_loop(0, XY - 1, start_qa, 0)
    lax.fori_loop(0, XY, start_core, 0)

    lax.fori_loop(8, 13, two_pieces(send_xy), 0)
    sum_plane()
    lax.fori_loop(13, 15, two_pieces(send_xy), 0)
    raw = meet(WA)
    waves(31, TB, WB)
    send_xy(30, raw)
    put_terms(m, meet(WB), XR.at[m])
    sum_cores()

    for n in later_loads:
        loads[n].wait()
    scr[...] = jnp.zeros_like(scr)
    TAB[0:ATOMS] = features
    for d in range(2):
        GS[d] = dot(pick(sx, d, 0), features).astype(bf16)
    ghost[0].start()
    ghost[1].start()

    scr2[...] = jnp.zeros_like(scr2)
    scr2[0:20, :] = win[...].astype(f32)
    wint_s[...] = scr2[...].T.astype(bf16)
    woutt_s[...] = wout[...].astype(f32).T.astype(bf16)
    gt_s[:, 0:128] = features.astype(f32).T.astype(bf16)
    slot_id = lax.broadcasted_iota(jnp.int32, (SLOTS, ATOMS), 0)
    swing, _ = cos_sin_turns(dist[...] * 0.1)
    env_s[...] = jnp.where(slot_id < cnt[...], 0.5 * (swing + 1.0), 0.0)

    centre = lax.broadcasted_iota(jnp.int32, (32, ATOMS), 0).astype(f32) * (5.0 / 19.0)
    table_row = lax.broadcasted_iota(jnp.int32, (2 * ATOMS, ATOMS), 0)
    sharpness = 0.02 * 19.0 * 19.0

    def message_step(i, running):
        base = i * GROUP
        basis, hot = [], []
        for u in range(GROUP):
            offset = dist[pl.ds(base + u, 1), :] - centre
            basis.append(jnp.exp(-sharpness * offset * offset).astype(bf16))
            hot.append(jnp.where(nbr[pl.ds(base + u, 1), :] == table_row, 1.0, 0.0).astype(bf16))
        for u in range(0, GROUP, 4):
            pre = dot(wint_s[:, 0:32], jnp.concatenate(basis[u : u + 4], axis=1))
            hidden = jnp.log(0.5 * jnp.exp(pre) + 0.5).astype(bf16)
            filters = dot(woutt_s[...], hidden)
            rows = dot(gt_s[...], jnp.concatenate(hot[u : u + 4], axis=1))
            both = filters * rows
            for v in range(4):
                running = running + env_s[pl.ds(base + u + v, 1), :] * both[:, v * 128 : (v + 1) * 128]
        return running

    ghost[0].wait_recv()
    ghost[1].wait_recv()
    scr[...] = jnp.zeros_like(scr)
    for d in range(2):
        rows = dot(pick(sy, d, 0), TAB[0:128]) + dot(pick(sy, d, 128)[:, 0:64], TAB[128:192])
        GS[2 + d] = rows.astype(bf16)
    ghost[2].start()
    ghost[3].start()

    xy_all.wait_recv()
    plane_mean = QS[2] * (1.0 / (2 * XY * ATOMS))
    for kb in range(KBS):
        totals = [jnp.zeros((C, 128), f32), jnp.zeros((C, 128), f32)]
        units = jnp.zeros((2, 128), f32)
        for j in range(XY):
            shift = QA[j] * (1.0 / ATOMS) - plane_mean
            parts = XR[j, TILES].astype(f32)
            unit = parts[4 * kb : 4 * kb + 2] + parts[4 * kb + 2 : 4 * kb + 4]
            units = units + unit
            for p in range(2):
                totals[p] = totals[p] + (
                    XR[j, 2 * kb + p].astype(f32) + shift * unit[p : p + 1]
                )
        ZS[kb, 0] = totals[0].astype(bf16)
        ZS[kb, 1] = totals[1].astype(bf16)
        ZS[kb, 2] = jnp.concatenate(
            [split_units(units), jnp.zeros((C - 4, 128), f32)], axis=0
        ).astype(bf16)

    def z_copy(i, slot):
        return rcopy(ZS.at[lax.rem(i, KBS)], ZR.at[slot], z_s, z_r, z_dev(i))

    z_all = rcopy(ZR.at[pl.ds(0, NZ - 1)], ZR.at[pl.ds(0, NZ - 1)], z_s, z_r, sib)

    def start_z(n, carry):
        z_copy(z_to(n), z).start()
        return carry

    lax.fori_loop(0, NZ - 1, start_z, 0)
    block = lax.rem(z, KBS)
    ZR[z] = ZS[block]
    QB[z] = QS[2]

    g_own = h * XY + m
    k_block = pl.multiple_of(g_own * PIECE + block * 128, 128)
    kt = wv[:, pl.ds(k_block, 128)].astype(f32)
    q2 = (TWO_PI * TWO_PI) * (
        kt[0:1] * kt[0:1] + kt[1:2] * kt[1:2] + 0.25 * (kt[2:3] * kt[2:3])
    )
    eye = lax.broadcasted_iota(jnp.int32, (C, C), 0) == lax.broadcasted_iota(jnp.int32, (C, C), 1)
    width = jnp.sum(jnp.where(eye, jnp.broadcast_to(fw[...], (C, C)), 0.0), axis=1, keepdims=True)
    wgt_s[...] = jnp.exp(-0.5 * (width * width) * q2) * ((TWO_PI * TWO_PI) / q2)

    ghost[2].wait_recv()
    ghost[3].wait_recv()
    gt_s[:, 128:256] = TAB[128:256].astype(f32).T.astype(bf16)
    messages = lax.fori_loop(0, SLOTS // GROUP, message_step, jnp.zeros((128, ATOMS), f32))
    message_rows = messages.astype(bf16).astype(f32).T.astype(bf16)
    base_s[...] = features.astype(f32) + dot(message_rows, wup[...])
    scr[...] = jnp.zeros_like(scr)
    scr2[...] = jnp.zeros_like(scr2)
    scr2[0:C, :] = wlong[...]

    qb_all.wait_recv()
    mean = QB[0]
    for j in range(1, NZ):
        mean = mean + QB[j]
    mean = mean * (1.0 / (GX * GY * ATOMS))
    QS[3] = mean

    qa_all.wait_send()
    qb_all.wait_send()
    qc_copy.wait_send()
    core_all.wait_send()
    xy_all.wait_send()
    for copy in ghost:
        copy.wait_send()

    z_all.wait_recv()
    totals = [jnp.zeros((C, 128), f32), jnp.zeros((C, 128), f32)]
    for j in range(NZ):
        shift = QB[j] * (1.0 / (2 * XY * ATOMS)) - mean
        parts = ZR[j, 2].astype(f32)
        for p in range(2):
            unit = parts[p : p + 1] + parts[2 + p : 3 + p]
            totals[p] = totals[p] + (ZR[j, p].astype(f32) + shift * unit)
    for p in range(2):
        FALL[g_own, block, p] = (totals[p] * wgt_s[...]).astype(bf16)

    def f_copy(delta, kb, slot):
        return rcopy(
            FALL.at[g_own, kb], FALL.at[g_own, kb], f_s.at[slot], f_r.at[kb],
            z_dev(wrap(z + delta)),
        )

    for n, delta in enumerate((2, 1, -1)):
        f_copy(delta, block, n).start()

    def block_of(turn):
        return lax.rem(block + turn + turn // 2 - 2 * (turn // 3), KBS)

    def a_copy(n, turn):
        kb = block_of(turn)
        return rcopy(
            FALL.at[g_own, kb], FALL.at[g_own, kb], a_s, a_r.at[turn * 4 + n // 4],
            xy_dev(xy_to(n)),
        )

    def b_copy(j, turn, group):
        kb = block_of(turn)
        return rcopy(
            FALL.at[h * XY + j, kb], FALL.at[h * XY + j, kb], b_s,
            b_r.at[turn * 4 + group], sib,
        )

    def send_block(turn):
        def start(n, carry):
            a_copy(n, turn).start()
            return carry

        lax.fori_loop(0, XY - 1, start, 0)
        b_copy(m, turn, 3).start()

    send_block(0)
    for turn in range(1, KBS):
        f_copy(1, block_of(turn), 0).wait_recv()
        send_block(turn)
    z_all.wait_send()
    for n in range(3):
        f_copy(1, block, n).wait_send()

    def project(half, group, turn, running):
        kb = block_of(turn)
        f0, f1, kf, w0, w1 = [], [], [], [], []
        for u in range(4):
            g = half * XY + xy_from(group * 4 + u)
            lanes = pl.ds(pl.multiple_of(kb * 128, 128), 128)
            f0.append(FALL[g, kb, 0])
            f1.append(FALL[g, kb, 1])
            kf.append(wv[:, pl.ds(pl.multiple_of(g * PIECE + kb * 128, 128), 128)])
            w0.append(W[g, 0, :, lanes])
            w1.append(W[g, 1, :, lanes])
        f0, f1, kf, w0, w1 = [jnp.concatenate(v, axis=1) for v in (f0, f1, kf, w0, w1)]
        kf = kf.astype(f32) * TWO_PI
        f0w, f1w = f0.astype(f32), f1.astype(f32)
        first, second = [f0], [f1]
        for d in range(3):
            first.append((kf[d : d + 1] * f1w).astype(bf16))
            second.append((-kf[d : d + 1] * f0w).astype(bf16))
        running = running + dot_nt(jnp.concatenate(first, axis=0), w0)
        return running + dot_nt(jnp.concatenate(second, axis=0), w1)

    def wait_near(step):
        turn, group = step // 4, lax.rem(step, 4)
        sem = a_r.at[step]

        @pl.when(group < 3)
        def _():
            rcopy(FALL.at[0], FALL.at[0], a_s, sem, sib).wait_recv()

        @pl.when(group == 3)
        def _():
            part = FALL.at[0, pl.ds(0, 3)]
            rcopy(part, part, a_s, sem, sib).wait_recv()

        for u in range(3):
            b_copy(xy_from(group * 4 + u), turn, group).start()

        @pl.when(group < 3)
        def _():
            b_copy(xy_from(group * 4 + 3), turn, group).start()

    def wait_other(step):
        rcopy(FALL.at[0], FALL.at[0], b_s, b_r.at[step], sib).wait_recv()

    def near(step, running):
        wait_near(step)
        return project(h, lax.rem(step, 4), step // 4, running)

    def other(step, running):
        wait_other(step)
        return project(1 - h, lax.rem(step, 4), step // 4, running)

    def both(step, running):
        wait_near(step)
        wait_other(step - LAG)
        running = project(h, lax.rem(step, 4), step // 4, running)
        return project(1 - h, lax.rem(step - LAG, 4), (step - LAG) // 4, running)

    fields = lax.fori_loop(0, LAG, near, jnp.zeros((4 * C, ATOMS), f32))
    fields = lax.fori_loop(LAG, 4 * KBS, both, fields)
    fields = lax.fori_loop(4 * KBS - LAG, 4 * KBS, other, fields)
    fields = fields * (1.0 / math.sqrt(GX * GY * ATOMS))

    centred = qf_s[...] - QS[3]
    for d in range(3):
        part = fields[(d + 1) * C : (d + 2) * C]
        frc_o[d : d + 1, :] = -FORCE_UNIT * jnp.sum(centred * part, axis=0, keepdims=True)
    scr[0:C, :] = fields[0:C]
    long_part = dot(scr[...].T, scr2[...], precision=lax.Precision.HIGHEST)
    upd_o[...] = (base_s[...] + long_part).astype(bf16)

    rest_a = FALL.at[pl.ds(0, XY - 1)]
    rcopy(rest_a, rest_a, a_s, a_r.at[0], sib).wait_send()
    rest_b = FALL.at[pl.ds(0, XY)]
    rcopy(rest_b, rest_b, b_s, b_r.at[0], sib).wait_send()


def per_device(*args):
    feat, pos, wv, fw, wch, win, wout, wup, wlong, sx, sy, nbr, cnt, dist = args
    operands = (
        feat, pos, wv, fw.reshape(1, C), wch.T, win, wout, wup, wlong, sx, sy, nbr,
        cnt.reshape(1, ATOMS), dist,
    )
    dma = pltpu.SemaphoreType.DMA
    scratch = [pltpu.VMEM(value.shape, value.dtype) for value in operands] + [
        pltpu.VMEM((PIECES, 2, ATOMS, PIECE), bf16),
        pltpu.VMEM((2, ATOMS, PIECE), bf16),
        pltpu.VMEM((2, ATOMS, PIECE), bf16),
        pltpu.VMEM((ATOMS, PIECE), f32),
        pltpu.VMEM((ATOMS, PIECE), f32),
        pltpu.VMEM((XY, 2, RAW, PIECE), f32),
        pltpu.VMEM((XY, 2, RAW, PIECE), f32),
        pltpu.VMEM((XY, TILES + 1, C, 128), bf16),
        pltpu.VMEM((XY, TILES + 1, C, 128), bf16),
        pltpu.VMEM((KBS, 3, C, 128), bf16),
        pltpu.VMEM((NZ, 3, C, 128), bf16),
        pltpu.VMEM((PIECES, KBS, 2, C, 128), bf16),
        pltpu.VMEM((4, C, 128), f32),
        pltpu.VMEM((XY, C, 128), f32),
        pltpu.VMEM((NZ, C, 128), f32),
        pltpu.VMEM((C, 128), f32),
        pltpu.VMEM((2 * ATOMS, 128), bf16),
        pltpu.VMEM((4, 32, 128), bf16),
        pltpu.VMEM((128, 128), f32),
        pltpu.VMEM((128, 128), f32),
        pltpu.VMEM((128, 128), f32),
        pltpu.VMEM((128, 128), bf16),
        pltpu.VMEM((32, ATOMS), bf16),
        pltpu.VMEM((C, ATOMS), f32),
        pltpu.VMEM((C, PIECE), f32),
        pltpu.VMEM((SLOTS, ATOMS), f32),
        pltpu.VMEM((C, 128), f32),
        pltpu.VMEM((128, 256), bf16),
        pltpu.VMEM((128, 128), bf16),
        pltpu.VMEM((128, 128), bf16),
        dma, dma, dma, dma, dma, dma,
        dma((4,)), dma((4,)),
        dma, dma((XY,)),
        dma, dma,
        dma, dma,
        dma((KBS,)), dma((KBS,)),
        dma, dma((4 * KBS,)),
        dma, dma((4 * KBS,)),
        dma((14,)),
    ]
    vmem = pl.BlockSpec(memory_space=pltpu.VMEM)
    return pl.pallas_call(
        kernel,
        out_shape=(
            jax.ShapeDtypeStruct((ATOMS, 128), bf16),
            jax.ShapeDtypeStruct((3, ATOMS), f32),
        ),
        in_specs=[pl.BlockSpec(memory_space=pl.ANY)] * 14,
        out_specs=(vmem, vmem),
        scratch_shapes=scratch,
        compiler_params=pltpu.CompilerParams(
            collective_id=0, has_side_effects=True, vmem_limit_bytes=56 * 1024 * 1024
        ),
    )(*operands)


def solution(mesh):
    atoms_first = P(("gx", "gy"), None)
    atoms_last = P(None, ("gx", "gy"))
    placed = (
        atoms_first, atoms_last, P(), P(), P(), P(), P(), P(), P(),
        atoms_last, atoms_last, atoms_last, P(("gx", "gy")), atoms_last,
    )
    return jax.shard_map(
        per_device,
        mesh=mesh,
        in_specs=placed,
        out_specs=(atoms_first, atoms_last),
        check_vma=False,
    )
```

time: 94 us -> 62.2 us (0.66)
  Pallas kernels: 84 us -> 59.4 us
  local copies, waits for them, and re-layouts: 8.72 us -> 1.96 us
    pallas_call x1, Pallas kernels: 84 us -> 59.4 us  [per_device(): pl.pallas_call(kernel, out_shape=(jax.ShapeDtypeStruct((ATOMS, 128), bf16...]
    unnamed x29 -> x4, local copies, waits for them, and re-layouts: 8.72 us -> 1.96 us
where the time goes in v2:
time: 62.2 us; the launch traced here: 62.1 us
  Pallas kernels  59.4 us (95%)
  local copies, waits for them, and re-layouts  1.96 us (3%)
  between operations  0.65 us (1%)
    pallas_call x1, Pallas kernels, per_device(): pl.pallas_call(kernel, out_shape=(jax.ShapeDtypeStruct((ATOMS, 128), bf16...  59.4 us
    unnamed x4, local copies, waits for them, and re-layouts  1.96 us

profile of v2, /device:TPU:1, one launch (start us, length us, event | category | flops | bytes accessed | tf_op | source)
XLA Modules:
  0.0 62.1 jit_solution(14040329806585601145)
XLA Ops:
  0.6 59.4 %shard_map.149 = (bf16[128,128]{1,0:T(8,128)(2,1)}, f32[3,128]{1,0:T(4,128)}) custom-call(bf16[128,128]{1,0:T(8,128)(2,1)} %refs_0_.1, f32[3,128]{1,0:T(4,128)} %refs_1_.1, s32[3,16384]{1,0:T(4,128)} %refs_2_.1, f32[1,16]{1,0:T(1,128)} %bitcast.4, bf16[16,128]{1,0:T(8,128)(2,1)} %bitcast.3, bf16[20,128]{1,0:T(8,128)(2,1)} %refs_5_.1, ...), custom_call_target="tpu_custom_call" | custom-call | tf_op jit(solution)/shard_map/pallas_call | solution.py:607
  60.1 0.0 copy-start
  60.1 1.4 %copy.18 = bf16[128,128]{1,0:T(8,128)(2,1)} copy(bf16[128,128]{1,0:T(8,128)(2,1)} %get-tuple-element.4) | data formatting | bytes 65536
  61.5 0.0 copy-done
  61.5 0.6 copy.19
Async XLA Ops:
  60.1 1.4 %copy-start = (f32[3,128]{1,0:T(4,128)S(1)}, f32[3,128]{1,0:T(4,128)}, u32[]{:S(2)}) copy-start(f32[3,128]{1,0:T(4,128)} %get-tuple-element.5) | copy-start | bytes 4612

commit v3 on v2

--- a/solution.py
+++ b/solution.py
@@ -25,7 +25,8 @@
 SLOTS = 64
 RAW = 24
 GROUP = 8
-LAG = 3
+CHIPS = 8
+STEPS = KBS * XY // CHIPS
 
 TWO_PI = 2.0 * math.pi
 FORCE_UNIT = 0.001
@@ -76,39 +77,43 @@
     gy = lax.axis_index("gy")
     h = lax.rem(gx, 2)
     z = gy // 2
-    m = (gx // 4) * 4 + lax.rem(gx // 2, 2) * 2 + lax.rem(gy, 2)
-
-    def xy_dev(i):
-        return ((i // 4) * 4 + lax.rem(i // 2, 2) * 2 + h, z * 2 + lax.rem(i, 2))
-
-    def z_dev(i):
-        return (gx, i * 2 + lax.rem(gy, 2))
-
+    row, column, xl = gx // 4, lax.rem(gx // 2, 2) * 2 + lax.rem(gy, 2), lax.rem(gy, 2)
+    m = row * 4 + column
     sib = (gx + 1 - 2 * h, gy)
 
-    def wrap(i):
-        return lax.rem(i + 2 * XY, XY)
-
-    def bend(a):
-        return lax.rem(2 + a + a // 2 + 2 * (a // 3), 4)
+    def wrap(i, size):
+        return jnp.where(i >= size, i - size, i)
+
+    rows_to = [wrap(row + d, 4) for d in range(4)]
+    rows_from = [rows_to[(4 - d) % 4] for d in range(4)]
+    columns_to = [wrap(column + d, 4) for d in range(4)]
+    columns_from = [columns_to[(4 - d) % 4] for d in range(4)]
+    high = [jnp.where(c >= 2, 1, 0) for c in columns_to]
+    device_x = [2 * high[d] + h for d in range(4)]
+    device_y = [2 * z + columns_to[d] - 2 * high[d] for d in range(4)]
+    far_first = (2, 3, 1, 0)
 
     def xy_to(n):
-        dy, dx = bend(n // 4), bend(lax.rem(n, 4))
-        return lax.rem(m // 4 + dy, 4) * 4 + lax.rem(lax.rem(m, 4) + dx, 4)
+        if isinstance(n, int):
+            return rows_to[far_first[n // 4]] * 4 + columns_to[far_first[n % 4]]
+        quarter = jnp.where(n >= 4, 1, 0) + jnp.where(n >= 8, 1, 0) + jnp.where(n >= 12, 1, 0)
+        rest = n - 4 * quarter
+        dy = jnp.where(quarter < 2, quarter + 2, 3 - quarter)
+        dx = jnp.where(rest < 2, rest + 2, 3 - rest)
+        return wrap(row + dy, 4) * 4 + wrap(column + dx, 4)
 
     def xy_from(n):
-        dy, dx = bend(n // 4), bend(lax.rem(n, 4))
-        return lax.rem(m // 4 + 4 - dy, 4) * 4 + lax.rem(lax.rem(m, 4) + 4 - dx, 4)
-
-    def far(n):
-        odd = lax.rem(n, 2)
-        return 8 + (1 - odd) * (n // 2) - odd * ((n + 1) // 2)
-
-    def z_to(n):
-        return lax.rem(z + far(n), NZ)
-
-    def z_from(n):
-        return lax.rem(z + NZ - far(n), NZ)
+        return rows_from[far_first[n // 4]] * 4 + columns_from[far_first[n % 4]]
+
+    def xy_dev(n):
+        dy, dx = far_first[n // 4], far_first[n % 4]
+        return (rows_to[dy] * 4 + device_x[dx], device_y[dx])
+
+    z_far = (8, 7, 9, 6, 10, 5, 11, 4, 12, 3, 13, 2, 14, 1, 15)
+    block = lax.rem(z, KBS)
+
+    def z_dev(d):
+        return (gx, 2 * wrap(z + d, NZ) + xl)
 
     x_up = (lax.rem(gx + 1, GX), gy)
     x_down = (lax.rem(gx + GX - 1, GX), gy)
@@ -126,12 +131,9 @@
     def greet(dev):
         pl.semaphore_signal(barrier, inc=1, device_id=dev, device_id_type=pl.DeviceIdType.MESH)
 
-    def greet_ring(i, carry):
-        greet(z_dev(z_to(i)))
-        greet(xy_dev(xy_to(i)))
-        return carry
-
-    lax.fori_loop(0, XY - 1, greet_ring, 0)
+    for n in range(XY - 1):
+        greet(z_dev(z_far[n]))
+        greet(xy_dev(n))
     greet(sib)
     for dev in (x_up, x_down, y_up, y_down):
         greet(dev)
@@ -158,7 +160,6 @@
     qe_s[...] = jnp.where(row_id == C, 1.0, padded).astype(bf16)
     own_sum = jnp.broadcast_to(jnp.sum(charges_t, axis=1, keepdims=True), (C, 128))
     QS[0] = own_sum
-    mean_s[...] = jnp.concatenate([own_sum * (1.0 / ATOMS)] * KBS, axis=1)
 
     lane_iota = lax.broadcasted_iota(jnp.int32, (ATOMS, 32), 0)
 
@@ -173,43 +174,41 @@
         rcopy(GS.at[3], TAB.at[pl.ds(224, 32)], g_s.at[3], g_r.at[3], y_down),
     ]
 
-    def qa_copy(i, slot):
-        return rcopy(QS.at[0], QA.at[slot], qa_s, qa_r, xy_dev(i))
+    qc_copy = rcopy(QS.at[0], QC, qc_s, qc_r, sib)
+
+    def qa_copy(n):
+        return rcopy(QS.at[1], QA.at[m], qa_s, qa_r, xy_dev(n))
 
     qa_all = rcopy(QA.at[pl.ds(0, XY - 1)], QA.at[pl.ds(0, XY - 1)], qa_s, qa_r, sib)
-    qc_copy = rcopy(QS.at[1], QC, qc_s, qc_r, sib)
-
-    def qb_copy(i, slot):
-        return rcopy(QS.at[2], QB.at[slot], qb_s, qb_r, z_dev(i))
+
+    def qb_copy(n):
+        return rcopy(QS.at[2], QB.at[z], qb_s, qb_r, z_dev(z_far[n]))
 
     qb_all = rcopy(QB.at[pl.ds(0, NZ - 1)], QB.at[pl.ds(0, NZ - 1)], qb_s, qb_r, sib)
 
-    def start_qa(n, carry):
-        qa_copy(xy_to(n), m).start()
-        return carry
+    def sum_pair():
+        qc_copy.wait_recv()
+        pair = QS[0] + QC[...]
+        QS[1] = pair
+        mean_s[...] = jnp.concatenate([pair * (1.0 / (2 * ATOMS))] * KBS, axis=1)
+
+        for n in range(XY - 1):
+            qa_copy(n).start()
 
     def sum_plane():
         qa_all.wait_recv()
-        QA[m] = QS[0]
+        QA[m] = QS[1]
         total = QA[0]
         for j in range(1, XY):
             total = total + QA[j]
-        QS[1] = total
-        qc_copy.start()
-
-    def sum_cores():
-        qc_copy.wait_recv()
-        QS[2] = QS[1] + QC[...]
-
-        def start(n, carry):
-            qb_copy(z_to(n), z).start()
-            return carry
-
-        lax.fori_loop(0, NZ - 1, start, 0)
+        QS[2] = total
+
+        for n in range(NZ - 1):
+            qb_copy(n).start()
 
     def piece_of(n):
         half = jnp.where(n < XY, 1 - h, h)
-        return half * XY + xy_to(lax.rem(n, XY))
+        return half * XY + xy_to(wrap(n, XY))
 
     def phases(n, turns):
         first = pl.multiple_of(piece_of(n) * PIECE, PIECE)
@@ -240,8 +239,8 @@
         CS[i, 0] = raw[0]
         CS[i, 1] = raw[1]
 
-    def xy_copy(i, slot):
-        return rcopy(XS.at[i], XR.at[slot], x_s, x_r, xy_dev(i))
+    def xy_copy(i, dev):
+        return rcopy(XS.at[i], XR.at[m], x_s, x_r, dev)
 
     xy_all = rcopy(XR.at[pl.ds(0, XY - 1)], XR.at[pl.ds(0, XY - 1)], x_s, x_r, sib)
 
@@ -266,9 +265,12 @@
         ).astype(bf16)
 
     def send_xy(n, raw):
-        i = xy_to(lax.rem(n, XY))
+        i = xy_to(wrap(n, XY))
         put_terms(i, raw, XS.at[i])
-        xy_copy(i, m).start()
+        y = jnp.where(i >= 4, 1, 0) + jnp.where(i >= 8, 1, 0) + jnp.where(i >= 12, 1, 0)
+        x = i - 4 * y
+        upper = jnp.where(x >= 2, 1, 0)
+        xy_copy(i, (4 * y + 2 * upper + h, 2 * z + x - 2 * upper)).start()
 
     def two_pieces(use):
         def body(step, carry):
@@ -296,17 +298,8 @@
         core_copy(xy_to(n)).start()
         return carry
 
-    lax.fori_loop(0, XY - 1, start_qa, 0)
-    lax.fori_loop(0, XY, start_core, 0)
-
-    lax.fori_loop(8, 13, two_pieces(send_xy), 0)
-    sum_plane()
-    lax.fori_loop(13, 15, two_pieces(send_xy), 0)
-    raw = meet(WA)
-    waves(31, TB, WB)
-    send_xy(30, raw)
-    put_terms(m, meet(WB), XR.at[m])
-    sum_cores()
+    qc_copy.start()
+    lax.fori_loop(0, 4, start_core, 0)
 
     for n in later_loads:
         loads[n].wait()
@@ -316,6 +309,17 @@
         GS[d] = dot(pick(sx, d, 0), features).astype(bf16)
     ghost[0].start()
     ghost[1].start()
+
+    sum_pair()
+    lax.fori_loop(4, XY, start_core, 0)
+
+    lax.fori_loop(8, 12, two_pieces(send_xy), 0)
+    sum_plane()
+    lax.fori_loop(12, 15, two_pieces(send_xy), 0)
+    raw = meet(WA)
+    waves(31, TB, WB)
+    send_xy(30, raw)
+    put_terms(m, meet(WB), XR.at[m])
 
     scr2[...] = jnp.zeros_like(scr2)
     scr2[0:20, :] = win[...].astype(f32)
@@ -356,39 +360,37 @@
     ghost[2].start()
     ghost[3].start()
 
+    qb_all.wait_recv()
+    QB[z] = QS[2]
+    mean = QB[0]
+    for j in range(1, NZ):
+        mean = mean + QB[j]
+    mean = mean * (1.0 / (GX * GY * ATOMS))
+    QS[3] = mean
     xy_all.wait_recv()
-    plane_mean = QS[2] * (1.0 / (2 * XY * ATOMS))
     for kb in range(KBS):
         totals = [jnp.zeros((C, 128), f32), jnp.zeros((C, 128), f32)]
-        units = jnp.zeros((2, 128), f32)
         for j in range(XY):
-            shift = QA[j] * (1.0 / ATOMS) - plane_mean
+            shift = QA[j] * (1.0 / (2 * ATOMS)) - mean
             parts = XR[j, TILES].astype(f32)
             unit = parts[4 * kb : 4 * kb + 2] + parts[4 * kb + 2 : 4 * kb + 4]
-            units = units + unit
             for p in range(2):
                 totals[p] = totals[p] + (
                     XR[j, 2 * kb + p].astype(f32) + shift * unit[p : p + 1]
                 )
         ZS[kb, 0] = totals[0].astype(bf16)
         ZS[kb, 1] = totals[1].astype(bf16)
-        ZS[kb, 2] = jnp.concatenate(
-            [split_units(units), jnp.zeros((C - 4, 128), f32)], axis=0
-        ).astype(bf16)
-
-    def z_copy(i, slot):
-        return rcopy(ZS.at[lax.rem(i, KBS)], ZR.at[slot], z_s, z_r, z_dev(i))
+
+    def z_copy(n):
+        return rcopy(
+            ZS.at[wrap(block + z_far[n] % KBS, KBS)], ZR.at[z], z_s, z_r, z_dev(z_far[n])
+        )
 
     z_all = rcopy(ZR.at[pl.ds(0, NZ - 1)], ZR.at[pl.ds(0, NZ - 1)], z_s, z_r, sib)
 
-    def start_z(n, carry):
-        z_copy(z_to(n), z).start()
-        return carry
-
-    lax.fori_loop(0, NZ - 1, start_z, 0)
-    block = lax.rem(z, KBS)
+    for n in range(NZ - 1):
+        z_copy(n).start()
     ZR[z] = ZS[block]
-    QB[z] = QS[2]
 
     g_own = h * XY + m
     k_block = pl.multiple_of(g_own * PIECE + block * 128, 128)
@@ -410,13 +412,6 @@
     scr2[...] = jnp.zeros_like(scr2)
     scr2[0:C, :] = wlong[...]
 
-    qb_all.wait_recv()
-    mean = QB[0]
-    for j in range(1, NZ):
-        mean = mean + QB[j]
-    mean = mean * (1.0 / (GX * GY * ATOMS))
-    QS[3] = mean
-
     qa_all.wait_send()
     qb_all.wait_send()
     qc_copy.wait_send()
@@ -428,47 +423,43 @@
     z_all.wait_recv()
     totals = [jnp.zeros((C, 128), f32), jnp.zeros((C, 128), f32)]
     for j in range(NZ):
-        shift = QB[j] * (1.0 / (2 * XY * ATOMS)) - mean
-        parts = ZR[j, 2].astype(f32)
         for p in range(2):
-            unit = parts[p : p + 1] + parts[2 + p : 3 + p]
-            totals[p] = totals[p] + (ZR[j, p].astype(f32) + shift * unit)
+            totals[p] = totals[p] + ZR[j, p].astype(f32)
     for p in range(2):
         FALL[g_own, block, p] = (totals[p] * wgt_s[...]).astype(bf16)
 
     def f_copy(delta, kb, slot):
         return rcopy(
             FALL.at[g_own, kb], FALL.at[g_own, kb], f_s.at[slot], f_r.at[kb],
-            z_dev(wrap(z + delta)),
+            z_dev(delta % NZ),
         )
 
     for n, delta in enumerate((2, 1, -1)):
         f_copy(delta, block, n).start()
 
     def block_of(turn):
-        return lax.rem(block + turn + turn // 2 - 2 * (turn // 3), KBS)
+        if isinstance(turn, int):
+            return wrap(block + (0, 1, 3, 2)[turn], KBS)
+        return wrap(block + jnp.where(turn < 2, turn, 5 - turn), KBS)
 
     def a_copy(n, turn):
         kb = block_of(turn)
         return rcopy(
-            FALL.at[g_own, kb], FALL.at[g_own, kb], a_s, a_r.at[turn * 4 + n // 4],
-            xy_dev(xy_to(n)),
+            FALL.at[g_own, kb], FALL.at[g_own, kb], a_s, a_r.at[turn * 2 + n // CHIPS],
+            xy_dev(n),
         )
 
     def b_copy(j, turn, group):
         kb = block_of(turn)
         return rcopy(
             FALL.at[h * XY + j, kb], FALL.at[h * XY + j, kb], b_s,
-            b_r.at[turn * 4 + group], sib,
+            b_r.at[turn * 2 + group], sib,
         )
 
     def send_block(turn):
-        def start(n, carry):
+        for n in range(XY - 1):
             a_copy(n, turn).start()
-            return carry
-
-        lax.fori_loop(0, XY - 1, start, 0)
-        b_copy(m, turn, 3).start()
+        b_copy(m, turn, 1).start()
 
     send_block(0)
     for turn in range(1, KBS):
@@ -481,8 +472,8 @@
     def project(half, group, turn, running):
         kb = block_of(turn)
         f0, f1, kf, w0, w1 = [], [], [], [], []
-        for u in range(4):
-            g = half * XY + xy_from(group * 4 + u)
+        for u in range(CHIPS):
+            g = half * XY + xy_from(group * CHIPS + u)
             lanes = pl.ds(pl.multiple_of(kb * 128, 128), 128)
             f0.append(FALL[g, kb, 0])
             f1.append(FALL[g, kb, 1])
@@ -496,57 +487,51 @@
         for d in range(3):
             first.append((kf[d : d + 1] * f1w).astype(bf16))
             second.append((-kf[d : d + 1] * f0w).astype(bf16))
-        running = running + dot_nt(jnp.concatenate(first, axis=0), w0)
-        return running + dot_nt(jnp.concatenate(second, axis=0), w1)
-
-    def wait_near(step):
-        turn, group = step // 4, lax.rem(step, 4)
-        sem = a_r.at[step]
-
-        @pl.when(group < 3)
-        def _():
-            rcopy(FALL.at[0], FALL.at[0], a_s, sem, sib).wait_recv()
-
-        @pl.when(group == 3)
-        def _():
-            part = FALL.at[0, pl.ds(0, 3)]
-            rcopy(part, part, a_s, sem, sib).wait_recv()
-
-        for u in range(3):
-            b_copy(xy_from(group * 4 + u), turn, group).start()
-
-        @pl.when(group < 3)
-        def _():
-            b_copy(xy_from(group * 4 + 3), turn, group).start()
-
-    def wait_other(step):
-        rcopy(FALL.at[0], FALL.at[0], b_s, b_r.at[step], sib).wait_recv()
-
-    def near(step, running):
-        wait_near(step)
-        return project(h, lax.rem(step, 4), step // 4, running)
-
-    def other(step, running):
-        wait_other(step)
-        return project(1 - h, lax.rem(step, 4), step // 4, running)
-
-    def both(step, running):
-        wait_near(step)
-        wait_other(step - LAG)
-        running = project(h, lax.rem(step, 4), step // 4, running)
-        return project(1 - h, lax.rem(step - LAG, 4), (step - LAG) // 4, running)
-
-    fields = lax.fori_loop(0, LAG, near, jnp.zeros((4 * C, ATOMS), f32))
-    fields = lax.fori_loop(LAG, 4 * KBS, both, fields)
-    fields = lax.fori_loop(4 * KBS - LAG, 4 * KBS, other, fields)
-    fields = fields * (1.0 / math.sqrt(GX * GY * ATOMS))
-
+        running = running + dot_nt(w0, jnp.concatenate(first, axis=0))
+        return running + dot_nt(w1, jnp.concatenate(second, axis=0))
+
+    def wait_near(turn, group):
+        chips = FALL.at[pl.ds(0, CHIPS - group), 0]
+        rcopy(chips, chips, a_s, a_r.at[turn * 2 + group], sib).wait_recv()
+        for u in range(CHIPS - group):
+            b_copy(xy_from(group * CHIPS + u), turn, group).start()
+
+    def wait_other(turn, group):
+        chips = FALL.at[pl.ds(0, CHIPS), 0]
+        rcopy(chips, chips, b_s, b_r.at[turn * 2 + group], sib).wait_recv()
+
+    def first_turn(running):
+        for group in range(2):
+            wait_near(0, group)
+            running = project(h, group, 0, running)
+        return running
+
+    def next_turn(turn, running):
+        for group in range(2):
+            wait_near(turn, group)
+            wait_other(turn - 1, group)
+            running = project(h, group, turn, running)
+            running = project(1 - h, group, turn - 1, running)
+        return running
+
+    def last_turn(running):
+        for group in range(2):
+            wait_other(KBS - 1, group)
+            running = project(1 - h, group, KBS - 1, running)
+        return running
+
+    fields = first_turn(jnp.zeros((ATOMS, 4 * C), f32))
+    fields = lax.fori_loop(1, KBS, next_turn, fields)
+    fields = last_turn(fields)
+
+    scr[:, 0 : 4 * C] = fields * (1.0 / math.sqrt(GX * GY * ATOMS))
+    columns = scr[...]
+    long_part = dot(columns, scr2[...], precision=lax.Precision.HIGHEST)
+    rows = columns.T
     centred = qf_s[...] - QS[3]
     for d in range(3):
-        part = fields[(d + 1) * C : (d + 2) * C]
+        part = rows[(d + 1) * C : (d + 2) * C]
         frc_o[d : d + 1, :] = -FORCE_UNIT * jnp.sum(centred * part, axis=0, keepdims=True)
-    scr[0:C, :] = fields[0:C]
-    long_part = dot(scr[...].T, scr2[...], precision=lax.Precision.HIGHEST)
     upd_o[...] = (base_s[...] + long_part).astype(bf16)
 
     rest_a = FALL.at[pl.ds(0, XY - 1)]
@@ -572,8 +557,8 @@
         pltpu.VMEM((XY, 2, RAW, PIECE), f32),
         pltpu.VMEM((XY, TILES + 1, C, 128), bf16),
         pltpu.VMEM((XY, TILES + 1, C, 128), bf16),
-        pltpu.VMEM((KBS, 3, C, 128), bf16),
-        pltpu.VMEM((NZ, 3, C, 128), bf16),
+        pltpu.VMEM((KBS, 2, C, 128), bf16),
+        pltpu.VMEM((NZ, 2, C, 128), bf16),
         pltpu.VMEM((PIECES, KBS, 2, C, 128), bf16),
         pltpu.VMEM((4, C, 128), f32),
         pltpu.VMEM((XY, C, 128), f32),
@@ -599,8 +584,8 @@
         dma, dma,
         dma, dma,
         dma((KBS,)), dma((KBS,)),
-        dma, dma((4 * KBS,)),
-        dma, dma((4 * KBS,)),
+        dma, dma((STEPS,)),
+        dma, dma((STEPS,)),
         dma((14,)),
     ]
     vmem = pl.BlockSpec(memory_space=pltpu.VMEM)

time: 62.2 us -> 57.7 us (0.928)
  Pallas kernels: 59.4 us -> 54.9 us
    pallas_call x1, Pallas kernels: 59.4 us -> 54.9 us  [per_device(): pl.pallas_call(kernel, out_shape=(jax.ShapeDtypeStruct((ATOMS, 128), bf16...]
where the time goes in v3:
time: 57.7 us; the launch traced here: 57.5 us
  Pallas kernels  54.9 us (95%)
  local copies, waits for them, and re-layouts  1.96 us (3%)
  between operations  0.65 us (1%)
    pallas_call x1, Pallas kernels, per_device(): pl.pallas_call(kernel, out_shape=(jax.ShapeDtypeStruct((ATOMS, 128), bf16...  54.9 us
    unnamed x4, local copies, waits for them, and re-layouts  1.96 us

profile of v3, /device:TPU:1, one launch (start us, length us, event | category | flops | bytes accessed | tf_op | source)
XLA Modules:
  0.0 57.5 jit_solution(7146765384706774810)
XLA Ops:
  0.6 54.9 %shard_map.149 = (bf16[128,128]{1,0:T(8,128)(2,1)}, f32[3,128]{1,0:T(4,128)}) custom-call(bf16[128,128]{1,0:T(8,128)(2,1)} %refs_0_.1, f32[3,128]{1,0:T(4,128)} %refs_1_.1, s32[3,16384]{1,0:T(4,128)} %refs_2_.1, f32[1,16]{1,0:T(1,128)} %bitcast.4, bf16[16,128]{1,0:T(8,128)(2,1)} %bitcast.3, bf16[20,128]{1,0:T(8,128)(2,1)} %refs_5_.1, ...), custom_call_target="tpu_custom_call" | custom-call | tf_op jit(solution)/shard_map/pallas_call | solution.py:592
  55.6 0.0 copy-start
  55.6 1.4 %copy.18 = bf16[128,128]{1,0:T(8,128)(2,1)} copy(bf16[128,128]{1,0:T(8,128)(2,1)} %get-tuple-element.4) | data formatting | bytes 65536
  57.0 0.0 copy-done
  57.0 0.6 %copy.19 = f32[3,128]{1,0:T(4,128)} copy(f32[3,128]{1,0:T(4,128)S(1)} %copy-done) | data formatting | bytes 3072
Async XLA Ops:
  55.6 1.4 %copy-start = (f32[3,128]{1,0:T(4,128)S(1)}, f32[3,128]{1,0:T(4,128)}, u32[]{:S(2)}) copy-start(f32[3,128]{1,0:T(4,128)} %get-tuple-element.5) | copy-start | bytes 4612

commit v4 on v3

--- a/solution.py
+++ b/solution.py
@@ -313,9 +313,13 @@
     sum_pair()
     lax.fori_loop(4, XY, start_core, 0)
 
-    lax.fori_loop(8, 12, two_pieces(send_xy), 0)
-    sum_plane()
-    lax.fori_loop(12, 15, two_pieces(send_xy), 0)
+    send_two = two_pieces(send_xy)
+
+    def own_half(step, carry):
+        pl.when(step == 12)(sum_plane)
+        return send_two(step, carry)
+
+    lax.fori_loop(8, 15, own_half, 0)
     raw = meet(WA)
     waves(31, TB, WB)
     send_xy(30, raw)
@@ -360,6 +364,21 @@
     ghost[2].start()
     ghost[3].start()
 
+    xy_all.wait_recv()
+    pieces = []
+    for kb in range(KBS):
+        totals = [jnp.zeros((C, 128), f32), jnp.zeros((C, 128), f32)]
+        units = jnp.zeros((2, 128), f32)
+        for j in range(XY):
+            parts = XR[j, TILES].astype(f32)
+            unit = parts[4 * kb : 4 * kb + 2] + parts[4 * kb + 2 : 4 * kb + 4]
+            units = units + unit
+            offset = QA[j] * (1.0 / (2 * ATOMS))
+            for p in range(2):
+                totals[p] = totals[p] + (
+                    XR[j, 2 * kb + p].astype(f32) + offset * unit[p : p + 1]
+                )
+        pieces.append((totals, units))
     qb_all.wait_recv()
     QB[z] = QS[2]
     mean = QB[0]
@@ -367,19 +386,9 @@
         mean = mean + QB[j]
     mean = mean * (1.0 / (GX * GY * ATOMS))
     QS[3] = mean
-    xy_all.wait_recv()
-    for kb in range(KBS):
-        totals = [jnp.zeros((C, 128), f32), jnp.zeros((C, 128), f32)]
-        for j in range(XY):
-            shift = QA[j] * (1.0 / (2 * ATOMS)) - mean
-            parts = XR[j, TILES].astype(f32)
-            unit = parts[4 * kb : 4 * kb + 2] + parts[4 * kb + 2 : 4 * kb + 4]
-            for p in range(2):
-                totals[p] = totals[p] + (
-                    XR[j, 2 * kb + p].astype(f32) + shift * unit[p : p + 1]
-                )
-        ZS[kb, 0] = totals[0].astype(bf16)
-        ZS[kb, 1] = totals[1].astype(bf16)
+    for kb, (totals, units) in enumerate(pieces):
+        for p in range(2):
+            ZS[kb, p] = (totals[p] - mean * units[p : p + 1]).astype(bf16)
 
     def z_copy(n):
         return rcopy(
@@ -457,7 +466,7 @@
         )
 
     def send_block(turn):
-        for n in range(XY - 1):
+        for n in reversed(range(XY - 1)):
             a_copy(n, turn).start()
         b_copy(m, turn, 1).start()
 
@@ -501,13 +510,13 @@
         rcopy(chips, chips, b_s, b_r.at[turn * 2 + group], sib).wait_recv()
 
     def first_turn(running):
-        for group in range(2):
+        for group in (1, 0):
             wait_near(0, group)
             running = project(h, group, 0, running)
         return running
 
     def next_turn(turn, running):
-        for group in range(2):
+        for group in (1, 0):
             wait_near(turn, group)
             wait_other(turn - 1, group)
             running = project(h, group, turn, running)
@@ -515,7 +524,7 @@
         return running
 
     def last_turn(running):
-        for group in range(2):
+        for group in (1, 0):
             wait_other(KBS - 1, group)
             running = project(1 - h, group, KBS - 1, running)
         return running

time: 57.7 us -> 57.2 us (level)
  no operation moved by 1% of the time
where the time goes in v4:
time: 57.2 us; the launch traced here: 57 us
  Pallas kernels  54.4 us (95%)
  local copies, waits for them, and re-layouts  1.96 us (3%)
  between operations  0.65 us (1%)
    pallas_call x1, Pallas kernels, per_device(): pl.pallas_call(kernel, out_shape=(jax.ShapeDtypeStruct((ATOMS, 128), bf16...  54.4 us
    unnamed x4, local copies, waits for them, and re-layouts  1.96 us

profile of v4, /device:TPU:1, one launch (start us, length us, event | category | flops | bytes accessed | tf_op | source)
XLA Modules:
  0.0 57.0 jit_solution(10953952387085936564)
XLA Ops:
  0.6 54.4 %shard_map.149 = (bf16[128,128]{1,0:T(8,128)(2,1)}, f32[3,128]{1,0:T(4,128)}) custom-call(bf16[128,128]{1,0:T(8,128)(2,1)} %refs_0_.1, f32[3,128]{1,0:T(4,128)} %refs_1_.1, s32[3,16384]{1,0:T(4,128)} %refs_2_.1, f32[1,16]{1,0:T(1,128)} %bitcast.4, bf16[16,128]{1,0:T(8,128)(2,1)} %bitcast.3, bf16[20,128]{1,0:T(8,128)(2,1)} %refs_5_.1, ...), custom_call_target="tpu_custom_call" | custom-call | tf_op jit(solution)/shard_map/pallas_call | solution.py:601
  55.0 0.0 copy-start
  55.1 1.4 %copy.18 = bf16[128,128]{1,0:T(8,128)(2,1)} copy(bf16[128,128]{1,0:T(8,128)(2,1)} %get-tuple-element.4) | data formatting | bytes 65536
  56.4 0.0 copy-done
  56.4 0.6 %copy.19 = f32[3,128]{1,0:T(4,128)} copy(f32[3,128]{1,0:T(4,128)S(1)} %copy-done) | data formatting | bytes 3072
Async XLA Ops:
  55.0 1.4 %copy-start = (f32[3,128]{1,0:T(4,128)S(1)}, f32[3,128]{1,0:T(4,128)}, u32[]{:S(2)}) copy-start(f32[3,128]{1,0:T(4,128)} %get-tuple-element.5) | copy-start | bytes 4612

commit v5 on v4

--- a/solution.py
+++ b/solution.py
@@ -62,7 +62,7 @@
 def kernel(*refs):
     sources, (upd_o, frc_o), held, rest = refs[:14], refs[14:16], refs[16:30], refs[30:]
     feat, pos, wv, fw, wch, win, wout, wup, wlong, sx, sy, nbr, cnt, dist = held
-    (W, WA, WB, TA, TB, CS, CR, XS, XR, ZS, ZR, FALL, QS, QA, QB, QC, TAB, GS,
+    (W, WA, WB, TA, TB, CS, CR, XS, XR, ZS, ZR, FALL, QS, QP, QA, QB, QC, TAB, GS,
     scr, scr2, base_s, xt_s, qe_s, qf_s, mean_s, env_s, wgt_s, gt_s, wint_s, woutt_s,
     qa_s, qa_r, qb_s, qb_r, qc_s, qc_r, g_s, g_r, c_s, c_r, x_s, x_r, z_s, z_r, f_s, f_r,
     a_s, a_r, b_s, b_r, in_sem) = rest
@@ -177,19 +177,26 @@
     qc_copy = rcopy(QS.at[0], QC, qc_s, qc_r, sib)
 
     def qa_copy(n):
-        return rcopy(QS.at[1], QA.at[m], qa_s, qa_r, xy_dev(n))
+        return rcopy(QP.at[0], QA.at[m], qa_s, qa_r, xy_dev(n))
 
     qa_all = rcopy(QA.at[pl.ds(0, XY - 1)], QA.at[pl.ds(0, XY - 1)], qa_s, qa_r, sib)
 
     def qb_copy(n):
-        return rcopy(QS.at[2], QB.at[z], qb_s, qb_r, z_dev(z_far[n]))
+        return rcopy(QP.at[1], QB.at[z], qb_s, qb_r, z_dev(z_far[n]))
 
     qb_all = rcopy(QB.at[pl.ds(0, NZ - 1)], QB.at[pl.ds(0, NZ - 1)], qb_s, qb_r, sib)
+
+    lower = lax.broadcasted_iota(jnp.int32, (C // 2, 128), 1) < 64
+
+    def unpack(packed):
+        return jnp.concatenate(
+            [jnp.broadcast_to(packed[:, n : n + 1], (C // 2, 128)) for n in (0, 64)], axis=0
+        )
 
     def sum_pair():
         qc_copy.wait_recv()
         pair = QS[0] + QC[...]
-        QS[1] = pair
+        QP[0] = jnp.where(lower, pair[0 : C // 2], pair[C // 2 : C])
         mean_s[...] = jnp.concatenate([pair * (1.0 / (2 * ATOMS))] * KBS, axis=1)
 
         for n in range(XY - 1):
@@ -197,11 +204,11 @@
 
     def sum_plane():
         qa_all.wait_recv()
-        QA[m] = QS[1]
+        QA[m] = QP[0]
         total = QA[0]
         for j in range(1, XY):
             total = total + QA[j]
-        QS[2] = total
+        QP[1] = total
 
         for n in range(NZ - 1):
             qb_copy(n).start()
@@ -366,6 +373,7 @@
 
     xy_all.wait_recv()
     pieces = []
+    offsets = [unpack(QA[j]) * (1.0 / (2 * ATOMS)) for j in range(XY)]
     for kb in range(KBS):
         totals = [jnp.zeros((C, 128), f32), jnp.zeros((C, 128), f32)]
         units = jnp.zeros((2, 128), f32)
@@ -373,18 +381,17 @@
             parts = XR[j, TILES].astype(f32)
             unit = parts[4 * kb : 4 * kb + 2] + parts[4 * kb + 2 : 4 * kb + 4]
             units = units + unit
-            offset = QA[j] * (1.0 / (2 * ATOMS))
             for p in range(2):
                 totals[p] = totals[p] + (
-                    XR[j, 2 * kb + p].astype(f32) + offset * unit[p : p + 1]
+                    XR[j, 2 * kb + p].astype(f32) + offsets[j] * unit[p : p + 1]
                 )
         pieces.append((totals, units))
     qb_all.wait_recv()
-    QB[z] = QS[2]
+    QB[z] = QP[1]
     mean = QB[0]
     for j in range(1, NZ):
         mean = mean + QB[j]
-    mean = mean * (1.0 / (GX * GY * ATOMS))
+    mean = unpack(mean) * (1.0 / (GX * GY * ATOMS))
     QS[3] = mean
     for kb, (totals, units) in enumerate(pieces):
         for p in range(2):
@@ -570,8 +577,9 @@
         pltpu.VMEM((NZ, 2, C, 128), bf16),
         pltpu.VMEM((PIECES, KBS, 2, C, 128), bf16),
         pltpu.VMEM((4, C, 128), f32),
-        pltpu.VMEM((XY, C, 128), f32),
-        pltpu.VMEM((NZ, C, 128), f32),
+        pltpu.VMEM((2, C // 2, 128), f32),
+        pltpu.VMEM((XY, C // 2, 128), f32),
+        pltpu.VMEM((NZ, C // 2, 128), f32),
         pltpu.VMEM((C, 128), f32),
         pltpu.VMEM((2 * ATOMS, 128), bf16),
         pltpu.VMEM((4, 32, 128), bf16),

time: 57.2 us -> 55.6 us (0.972)
  Pallas kernels: 54.4 us -> 52.8 us
    pallas_call x1, Pallas kernels: 54.4 us -> 52.8 us  [per_device(): pl.pallas_call(kernel, out_shape=(jax.ShapeDtypeStruct((ATOMS, 128), bf16...]
where the time goes in v5:
time: 55.6 us; the launch traced here: 55.4 us
  Pallas kernels  52.8 us (95%)
  local copies, waits for them, and re-layouts  1.96 us (4%)
  between operations  0.65 us (1%)
    pallas_call x1, Pallas kernels, per_device(): pl.pallas_call(kernel, out_shape=(jax.ShapeDtypeStruct((ATOMS, 128), bf16...  52.8 us
    unnamed x4, local copies, waits for them, and re-layouts  1.96 us

profile of v5, /device:TPU:1, one launch (start us, length us, event | category | flops | bytes accessed | tf_op | source)
XLA Modules:
  0.0 55.4 jit_solution(10001666021180332955)
XLA Ops:
  0.6 52.8 %shard_map.149 = (bf16[128,128]{1,0:T(8,128)(2,1)}, f32[3,128]{1,0:T(4,128)}) custom-call(bf16[128,128]{1,0:T(8,128)(2,1)} %refs_0_.1, f32[3,128]{1,0:T(4,128)} %refs_1_.1, s32[3,16384]{1,0:T(4,128)} %refs_2_.1, f32[1,16]{1,0:T(1,128)} %bitcast.4, bf16[16,128]{1,0:T(8,128)(2,1)} %bitcast.3, bf16[20,128]{1,0:T(8,128)(2,1)} %refs_5_.1, ...), custom_call_target="tpu_custom_call" | custom-call | tf_op jit(solution)/shard_map/pallas_call | solution.py:609
  53.4 0.0 copy-start
  53.4 1.4 %copy.18 = bf16[128,128]{1,0:T(8,128)(2,1)} copy(bf16[128,128]{1,0:T(8,128)(2,1)} %get-tuple-element.4) | data formatting | bytes 65536
  54.8 0.0 copy-done
  54.8 0.6 %copy.19 = f32[3,128]{1,0:T(4,128)} copy(f32[3,128]{1,0:T(4,128)S(1)} %copy-done) | data formatting | bytes 3072
Async XLA Ops:
  53.4 1.4 %copy-start = (f32[3,128]{1,0:T(4,128)S(1)}, f32[3,128]{1,0:T(4,128)}, u32[]{:S(2)}) copy-start(f32[3,128]{1,0:T(4,128)} %get-tuple-element.5) | copy-start | bytes 4612
